TPU v7x, 512 devices: a whole 4x4x16 slice. The times are simulated.
512 devices in a mesh: seq: 16 (over z), mp: 8 (over x, core), dp: 4 (over y).
Axes of the slice: x: 4, y: 4, z: 16, core: 2. Of those that a mesh axis runs over, the one named last changes fastest.
Arguments:
- tokens: bfloat16 [4, 4096, 768], P('dp', 'seq'), may hold values from -6 to 6
- gain: float32 [768], replicated, may hold values from 0.5 to 1.5
- qkv_weight: bfloat16 [768, 3, 768], P(None, None, 'mp'), may hold values from -12 to 12
- out_weight: bfloat16 [768, 768], P('mp'), may hold values from -0.21875 to 0.21875
- counts: int32 [4], P('dp'), may hold values from 1 to 4096, 10240 in all
- grad_out: bfloat16 [4, 4096, 768], P('dp', 'seq'), may hold values from -6 to 6
Outputs:
- d_tokens: bfloat16 [4, 4096, 768], P('dp', 'seq', 'mp')
- d_qkv_weight: float32 [768, 3, 768], P(('seq', 'dp'), None, 'mp')
- d_out_weight: float32 [768, 768], P('mp', ('seq', 'dp'))
- d_gain: float32 [768], P('mp')
All inputs are finite; a program needn't handle non-finite values. No bound on the sum of `counts` on one device may be relied on, other than what follows from the above.
Results may differ from a plain program's by a relative error of at most 0.02.
The roundings to bfloat16 on the way count: a program that leaves them out, or rounds other values in their place, can miss the bound.
Values may be sent and summed in bfloat16 or wider, within the bound.
A program may use at most 64 MiB of HBM per device.

v0:
```python
import math

import jax
import jax.numpy as jnp
from jax import lax
from jax.sharding import PartitionSpec as P

HDIM = 48
DILATION_RATE = 2


far_below = -1e30


def for_sending(array):

    def short(part):
        return part.astype(jnp.bfloat16) if part.dtype == jnp.float32 else part

    return jax.tree.map(short, array)


def contract(form, left_op, right_op):
    return jnp.einsum(form, left_op, right_op, preferred_element_type=jnp.float32)


def pick_rows(value_array):
    count_heads, slide_length = (value_array.shape[0], value_array.shape[1])
    trailing_part = value_array.shape[2:]
    folded_key = value_array.reshape(
        (count_heads // DILATION_RATE, DILATION_RATE, slide_length // DILATION_RATE, DILATION_RATE)
        + trailing_part
    )
    picked_rows = jnp.diagonal(folded_key, axis1=1, axis2=3)
    picked_rows = jnp.moveaxis(picked_rows, -1, 1)
    return picked_rows.reshape((count_heads, slide_length // DILATION_RATE) + trailing_part)


def insert_rows(value_array, slide_length):
    count_heads = value_array.shape[0]
    trailing_part = value_array.shape[2:]
    folded_key = value_array.reshape(
        (count_heads // DILATION_RATE, DILATION_RATE, slide_length // DILATION_RATE, 1)
        + trailing_part
    )
    index_rows = lax.broadcasted_iota(jnp.int32, (DILATION_RATE, DILATION_RATE), 0)
    column_index = lax.broadcasted_iota(jnp.int32, (DILATION_RATE, DILATION_RATE), 1)
    identity_matrix = (index_rows == column_index).astype(value_array.dtype)
    identity_matrix = identity_matrix.reshape(
        (1, DILATION_RATE, 1, DILATION_RATE) + (1,) * len(trailing_part)
    )
    return (folded_key * identity_matrix).reshape((count_heads, slide_length) + trailing_part)


def attend_block(
    queries, keys_near, values_near, keys_far, values_far, grad_attend, live_rows, live_far
):
    count_heads, slide_length, depth = queries.shape
    scaling = 1.0 / math.sqrt(depth)
    near_score = jnp.where(
        live_rows[None, None, :], contract("hqe,hke->hqk", queries, keys_near) * scaling, far_below
    )
    far_queries = pick_rows(queries)
    far_score = jnp.where(
        live_far[:, None, :], contract("hqe,hke->hqk", far_queries, keys_far) * scaling, far_below
    )
    near_top = jnp.max(near_score, axis=2)
    far_top = jnp.maximum(pick_rows(near_top), jnp.max(far_score, axis=2))
    selected_rows = (
        insert_rows(
            jnp.ones((count_heads, slide_length // DILATION_RATE), jnp.float32), slide_length
        )
        > 0.5
    )
    row_top = jnp.where(selected_rows, insert_rows(far_top, slide_length), near_top)
    near_exp = jnp.exp(near_score - row_top[:, :, None])
    far_exp = jnp.exp(far_score - far_top[:, :, None])
    totals = jnp.sum(near_exp, axis=2) + insert_rows(jnp.sum(far_exp, axis=2), slide_length)
    live_grid = jnp.broadcast_to(live_rows[None, :], (count_heads, slide_length))
    near_weight = jnp.where(live_grid[:, :, None], near_exp / totals[:, :, None], 0.0)
    far_weight = jnp.where(
        pick_rows(live_grid)[:, :, None], far_exp / pick_rows(totals)[:, :, None], 0.0
    )
    near_bar = near_weight.astype(jnp.bfloat16)
    far_bar = far_weight.astype(jnp.bfloat16)
    attended = contract("hqk,hke->hqe", near_bar, values_near)
    attended = attended + insert_rows(contract("hqk,hke->hqe", far_bar, values_far), slide_length)
    attended = attended.astype(jnp.bfloat16)
    far_grad = pick_rows(grad_attend)
    near_prob = contract("hqe,hke->hqk", grad_attend, values_near)
    far_prob = contract("hqe,hke->hqk", far_grad, values_far)
    deltas = jnp.sum(near_weight * near_prob, axis=2) + insert_rows(
        jnp.sum(far_weight * far_prob, axis=2), slide_length
    )
    near_ds = (near_weight * (near_prob - deltas[:, :, None]) * scaling).astype(jnp.bfloat16)
    far_ds = (far_weight * (far_prob - pick_rows(deltas)[:, :, None]) * scaling).astype(
        jnp.bfloat16
    )
    d_query = contract("hqk,hke->hqe", near_ds, keys_near)
    d_query = d_query + insert_rows(contract("hqk,hke->hqe", far_ds, keys_far), slide_length)
    d_key = contract("hqk,hqe->hke", near_ds, queries)
    d_value = contract("hqk,hqe->hke", near_bar, grad_attend)
    far_dkey = contract("hqk,hqe->hke", far_ds, far_queries)
    far_dvalue = contract("hqk,hqe->hke", far_bar, far_grad)
    return (attended, d_query, d_key, d_value, far_dkey, far_dvalue)


def per_device(tokens, gain, qkv_weight, out_weight, counts, grad_out):
    slide_tokens = tokens[0]
    slide_grad = grad_out[0]
    slide_count = counts[0]
    slide_length = slide_tokens.shape[0]
    group_width = qkv_weight.shape[2]
    count_heads = group_width // HDIM
    sequence_count = lax.axis_size("seq")
    sparse_length = slide_length // DILATION_RATE * sequence_count
    widened = slide_tokens.astype(jnp.float32)
    centered = widened - jnp.mean(widened, axis=1, keepdims=True)
    inverse_std = lax.rsqrt(jnp.mean(centered * centered, axis=1, keepdims=True) + 1e-05)
    normal_form = centered * inverse_std
    normed = (normal_form * gain[None, :]).astype(jnp.bfloat16)
    projected = jnp.einsum(
        "td,dcf->tcf", normed, qkv_weight, preferred_element_type=jnp.float32
    ).astype(jnp.bfloat16)
    split_heads = projected.reshape(slide_length, 3, count_heads, HDIM).transpose(1, 2, 0, 3)
    queries, keys_here, values_here = (split_heads[0], split_heads[1], split_heads[2])
    grad_attend = jnp.einsum(
        "td,fd->tf", slide_grad, out_weight, preferred_element_type=jnp.float32
    ).astype(jnp.bfloat16)
    grad_attend = grad_attend.reshape(slide_length, count_heads, HDIM).transpose(1, 0, 2)
    first_row = lax.axis_index("seq") * slide_length
    positions = first_row + lax.broadcasted_iota(jnp.int32, (slide_length,), 0)
    live_rows = positions < slide_count
    sparse_positions = (
        lax.broadcasted_iota(jnp.int32, (count_heads, sparse_length), 1) * DILATION_RATE
    )
    sparse_positions = (
        sparse_positions
        + lax.broadcasted_iota(jnp.int32, (count_heads, sparse_length), 0) % DILATION_RATE
    )
    live_far = sparse_positions < slide_count
    outgoing = jnp.stack([pick_rows(keys_here), pick_rows(values_here)])
    gathered = lax.all_gather(for_sending(outgoing), "seq", axis=2, tiled=True).astype(
        outgoing.dtype
    )
    results = attend_block(
        queries, keys_here, values_here, gathered[0], gathered[1], grad_attend, live_rows, live_far
    )
    far_terms = jnp.stack([results[4], results[5]])
    owned = lax.psum_scatter(
        far_terms.astype(jnp.bfloat16), "seq", scatter_dimension=2, tiled=True
    ).astype(jnp.float32)
    d_key = results[2] + insert_rows(owned[0], slide_length)
    d_value = results[3] + insert_rows(owned[1], slide_length)
    d_proj = jnp.stack([results[1], d_key, d_value]).astype(jnp.bfloat16)
    d_proj = d_proj.transpose(2, 0, 1, 3).reshape(slide_length, 3, group_width)
    attended = results[0].transpose(1, 0, 2).reshape(slide_length, group_width)
    out_term = jnp.einsum("td,tf->df", slide_grad, attended, preferred_element_type=jnp.float32)
    qkv_term = jnp.einsum("td,tcf->dcf", normed, d_proj, preferred_element_type=jnp.float32)
    qkv_share, out_share = (
        lax.psum_scatter(qkv_term, ("seq", "dp"), scatter_dimension=0, tiled=True),
        lax.psum_scatter(out_term, ("seq", "dp"), scatter_dimension=0, tiled=True),
    )
    d_out_weight = out_share.T
    normed_part = jnp.einsum("tcf,dcf->td", d_proj, qkv_weight, preferred_element_type=jnp.float32)
    column = lax.axis_index("mp") * group_width
    d_normed = lax.psum(normed_part.astype(jnp.bfloat16), "mp").astype(jnp.float32)
    scaled = d_normed * gain[None, :]
    mean_scaled = jnp.mean(scaled, axis=1, keepdims=True)
    mean_mixed = jnp.mean(scaled * normal_form, axis=1, keepdims=True)
    full_grad = (
        slide_grad.astype(jnp.float32)
        + (scaled - mean_scaled - normal_form * mean_mixed) * inverse_std
    )
    d_tokens = lax.dynamic_slice_in_dim(full_grad, column, group_width, 1).astype(jnp.bfloat16)
    gain_term = jnp.sum(
        lax.dynamic_slice_in_dim(d_normed * normal_form, column, group_width, 1), axis=0
    )
    d_gain = lax.psum(gain_term, ("seq", "dp"))
    return (d_tokens[None], qkv_share, d_out_weight, d_gain)


def solution(mesh):
    placed = (
        P("dp", "seq", None),
        P(),
        P(None, None, "mp"),
        P("mp", None),
        P("dp"),
        P("dp", "seq", None),
    )
    return jax.shard_map(
        per_device,
        mesh=mesh,
        in_specs=placed,
        out_specs=(
            P("dp", "seq", "mp"),
            P(("seq", "dp"), None, "mp"),
            P("mp", ("seq", "dp")),
            P("mp"),
        ),
        check_vma=False,
    )
```

profile of v0, /device:TPU:1, one launch (start us, length us, event | category | flops | bytes accessed | tf_op | source)
XLA Modules:
  0.0 514.6 jit_solution(14523833871862101041)
XLA Ops:
  7.3 1.2 convert_reduce_fusion
  8.5 1.2 fusion.16
  9.7 1.4 fusion.24
  11.7 0.6 gather_fusion.2
  12.3 0.6 gather_fusion.3
  12.9 36.3 %all_gather.3 = bf16[2,2,2048,48]{2,3,1,0:T(8,128)(2,1)} all-gather(bf16[2,2,128,48]{2,3,1,0:T(8,128)(2,1)S(1)} %pad_maximum_fusion.2), channel_id=1, replica_groups=mesh['seq'=16,'mp'=8,'dp'=4] {'seq'}, dimensions={2}, use_global_device_ids=true | all-gather | bytes 835584 | tf_op jit(solution)/shard_map/all_gather | solution.py:143
  49.4 0.6 gather_fusion.1
  51.2 0.6 gather_fusion
  51.9 1.6 fusion.61
  53.5 0.4 fusion.3
  53.9 0.8 mul.301
  54.7 1.0 mul.302
  55.7 0.7 mul.296
  56.4 1.0 mul.297
  57.6 0.8 reduce_sum.90
  58.4 1.0 copy.56
  59.4 0.6 gather_fusion.5
  60.1 0.6 gather_fusion.4
  60.7 1.2 convolution_convert_fusion.2
  62.1 0.6 gather_fusion.6
  62.7 3.1 multiply_reduce_fusion
  65.8 1.4 fusion.2
  67.4 1.1 multiply_reduce_fusion.2
  68.8 0.6 gather_fusion.7
  69.4 2.3 multiply_convert_fusion
  72.1 0.7 copy-done.2
  72.8 0.9 pad_maximum_fusion
  73.7 5.9 %copy.90 = bf16[2,2,2048,48]{3,1,0,2:T(2,128)(2,1)} copy(bf16[2,2,2048,48]{2,3,1,0:T(8,128)(2,1)} %pad_maximum_fusion) | data formatting | bytes 1572864
  79.6 5.4 %reshape.389 = bf16[2048,192]{1,0:T(8,128)(2,1)} reshape(bf16[2048,2,2,48]{3,2,1,0:T(2,128)(2,1)} %bitcast.178) | data formatting | bytes 1572864
  85.1 1.6 fusion.20
  87.2 1.7 fusion.32
  89.7 0.4 copy-done.4
  90.1 0.9 convolution_bitcast_fusion.1
  91.0 57.5 %reduce-scatter.6.cloned.1.call-done = bf16[128,192]{1,0:T(8,128)(2,1)} async-done(((bf16[2048,192]{1,0:T(8,128)(2,1)}), bf16[128,192]{1,0:T(8,128)(2,1)}) %reduce-scatter.6.cloned.1.call-update) | async-done | bytes 49168
  148.5 1.0 reshape.390
  150.7 1.1 fusion.4
  152.0 1.6 fusion.26
  153.6 1.3 dynamic-slice
  155.5 78.4 %all-reduce.6.cloned.1.call-done = bf16[256,768]{1,0:T(8,128)(2,1)} async-done(((bf16[256,768]{1,0:T(8,128)(2,1)}), bf16[256,768]{1,0:T(8,128)(2,1)}) %all-reduce.6.cloned.1.call-update) | async-done | bytes 393232 | tf_op jit(solution)/shard_map/psum | solution.py:167
  234.0 1.0 convert_element_type.102
  235.0 1.3 fusion.34
  236.7 0.7 copy.73
  237.4 116.7 %psum.15 = f32[96]{0:T(128)} all-reduce(f32[96]{0:T(128)S(1)} %get-tuple-element.20), channel_id=1, replica_groups=mesh['seq'=16,'mp'=8,'dp'=4] {'seq','dp'}, use_global_device_ids=true, to_apply=%region_15.16 | all-reduce | flops 96 | bytes 768 | tf_op jit(solution)/shard_map/psum | solution.py:179
  354.2 150.8 %all-reduce.8.cloned.1.call-done = (f32[768,3,96]{2,0,1:T(8,128)}, f32[768,96]{0,1:T(8,128)}) async-done(((f32[768,3,96]{2,0,1:T(8,128)}, f32[768,96]{0,1:T(8,128)}), (f32[768,3,96]{2,0,1:T(8,128)}, f32[768,96]{0,1:T(8,128)})) %all-reduce.8.cloned.1.call-update) | async-done | bytes 1179664
  505.0 1.0 dynamic-slice_bitcast_fusion
  506.0 0.7 copy.75
  506.6 0.8 constant_dynamic-slice_fusion
  507.4 0.6 copy.74
  (113 shorter events, 5.4 us)
Async XLA Ops:
  7.2 2.6 copy-start
  7.2 141.4 %reduce-scatter.6.cloned.1.call-start = ((), (), s32[]{:S(2)}) async-start(), calls=%async_computation.2 | async-start | bytes 1114112
  7.3 52.1 %copy-start.20 = (f32[2,2]{1,0:T(2,128)}, f32[2,2]{1,0:T(2,128)S(1)}, u32[]{:S(2)}) copy-start(f32[2,2]{1,0:T(2,128)S(1)} %compare_convert_fusion) | copy-start | bytes 52
  8.5 3.8 copy-start.14
  9.7 2.5 copy-start.12
  11.2 39.4 %copy-start.5 = (bf16[256,3,96]{0,2,1:T(8,128)(2,1)}, bf16[256,3,96]{0,2,1:T(8,128)(2,1)S(1)}, u32[]{:S(2)}) copy-start(bf16[256,3,96]{0,2,1:T(8,128)(2,1)S(1)} %convert_element_type.93) | copy-start | bytes 442372
  50.7 1.1 copy-start.22
  53.5 7.2 %copy-start.3 = (bf16[1,256,768]{2,1,0:T(8,128)(2,1)S(1)}, bf16[1,256,768]{2,1,0:T(8,128)(2,1)}, u32[]{:S(2)}) copy-start(bf16[1,256,768]{2,1,0:T(8,128)(2,1)} %param.11) | copy-start | bytes 1179652
  53.5 4.9 copy-start.16
  53.9 6.1 %copy-start.18 = (f32[2,128]{1,0:T(2,128)}, f32[2,128]{1,0:T(2,128)S(1)}, u32[]{:S(2)}) copy-start(f32[2,128]{1,0:T(2,128)S(1)} %fusion.3) | copy-start | bytes 3076
  57.6 1.8 copy-start.9
  62.7 3.1 copy-start.17
  65.8 1.4 copy-start.19
  65.8 1.6 copy-start.10
  65.8 1.6 copy-start.6
  65.8 1.6 copy-start.23
  67.1 1.6 copy-start.21
  69.4 3.4 copy-start.8
  71.8 1.0 copy-start.2
  85.0 149.0 %all-reduce.6.cloned.1.call-start = ((), (), s32[]{:S(2)}) async-start(), calls=%async_computation.1 | async-start | bytes 786432 | tf_op jit(solution)/shard_map/psum | solution.py:167
  86.7 2.4 copy-start.7
  89.1 1.0 copy-start.4
  150.4 1.5 copy-start.1
  150.5 1.5 copy-start.11
  150.5 1.5 copy-start.13
  150.5 1.5 copy-start.15
  151.9 353.1 %all-reduce.8.cloned.1.call-start = ((), (), s32[]{:S(2)}) async-start(), calls=%async_computation.3 | async-start | bytes 2949120
Sparse Core Ops, SparseCore 0:
  85.1 63.3 reduce-scatter.5
  152.0 81.9 all-reduce.5
  237.4 267.5 all-reduce.7
where the time goes:
time: 524 us; the launch traced here: 515 us
  waiting for transfers between devices  287 us (55%)
  blocking collectives  153 us (29%)
  local copies, waits for them, and re-layouts  31.3 us (6%)
  matrix products  18 us (3%)
  between operations  15.8 us (3%)
  other arithmetic  9.45 us (2%)
    unnamed x5, waiting for transfers between devices  208 us
    psum x1, blocking collectives, per_device(): d_gain = lax.psum(gain_term, ('seq', 'dp'))  117 us
    psum x1, waiting for transfers between devices, per_device(): lax.psum(normed_part.astype(jnp.bfloat16), 'mp').astype(jnp.float32)  78.4 us
    all_gather x1, blocking collectives, per_device(): lax.all_gather(for_sending(outgoing), 'seq', axis=2, tiled=True)  36.3 us
    unnamed x57, local copies, waits for them, and re-layouts  17.6 us
    dot_general x12, matrix products, contract(): jnp.einsum(form, left_op, right_op, preferred_element_type=jnp.float32)  11.8 us
  transfers between devices with their start and end apart: 3, of which 3 were waited for; matrix products, arithmetic and copies ran while one was open for 2% of the time, Pallas kernels for 0%

commit v1 on v0

v1 whole, which is shorter than its diff:
```python
import functools
import math

import jax
import jax.numpy as jnp
from jax import lax
from jax.experimental import pallas as pl
from jax.experimental.pallas import tpu as pltpu
from jax.sharding import PartitionSpec as P

HDIM = 48
BLOCK = 256
HALF = BLOCK // 2
GROUP = 2 * HDIM
LANES = 128
MESH = pl.DeviceIdType.MESH
BF = jnp.bfloat16
F32 = jnp.float32
far_below = -1e30


def dot_nn(left, right):
    return lax.dot_general(left, right, (((1,), (0,)), ((), ())), preferred_element_type=F32)


def dot_nt(left, right):
    return lax.dot_general(left, right, (((1,), (1,)), ((), ())), preferred_element_type=F32)


def iota(shape, axis):
    return lax.broadcasted_iota(jnp.int32, shape, axis)


def one_hot(condition):
    return jnp.where(condition, 1.0, 0.0).astype(BF)


def row_sum(value):
    return jnp.sum(value, axis=1, keepdims=True)


def floor_div(value, by):
    return jnp.floor((value + 0.5) * (1.0 / by))


def layer_kernel(
    n_seq, n_mp, n_dp,
    counts, tokens, grad_out, gain, weight, out_weight,
    tok_out, early_out, late_out, gain_out,
    kv_far, scores, probs, top, kv_here, q_here, da_here, q_rows, da_rows,
    near_scores, near_probs, normed_s, go_s, normed_p, go_p, gain_pad, mixed_pad, weight_pad,
    contrib, far_send, far_recv, d_parts, own_parts,
    y_send, y_recv, z_send, z_recv, mp_send, mp_recv, gy_send, gy_recv, gz_send, gz_recv,
    ag_ss, ag_rs, rs_ss, rs_rs, y_ss, y_rs, z_ss, z_rs, mp_ss, mp_rs, gy_ss, gy_rs, gz_ss, gz_rs,
):
    width = n_mp * GROUP
    chunk = width // n_dp
    rows = chunk // n_seq
    rows_pad = -(-rows // 16) * 16
    mid = n_seq // 2
    scaling = 1.0 / math.sqrt(HDIM)
    s_me = lax.axis_index("seq")
    m_me = lax.axis_index("mp")
    d_me = lax.axis_index("dp")
    count = counts[0]

    def peer(axis, me, size, step):
        return {axis: lax.rem(me + (step + size), size)}

    barrier = pltpu.get_barrier_semaphore()
    for axis, me, size in (("seq", s_me, n_seq), ("dp", d_me, n_dp), ("mp", m_me, n_mp)):
        for step in range(1, size):
            pl.semaphore_signal(
                barrier, inc=1, device_id=peer(axis, me, size, step), device_id_type=MESH
            )

    def remote(src, dst, send, recv, device):
        return pltpu.make_async_remote_copy(
            src_ref=src, dst_ref=dst, send_sem=send, recv_sem=recv,
            device_id=device, device_id_type=MESH,
        )

    def position(shape, axis):
        at = iota(shape, axis)
        return 2 * (at % HALF) + at // HALF

    order = one_hot(position((BLOCK, BLOCK), 0) == iota((BLOCK, BLOCK), 1))
    eye = one_hot(iota((BLOCK, BLOCK), 0) == iota((BLOCK, BLOCK), 1))

    x = dot_nn(order, tokens[...])
    mean = row_sum(x) * (1.0 / width)
    centered = x - mean
    inverse_std = lax.rsqrt(row_sum(centered * centered) * (1.0 / width) + 1e-05)
    normal_form = centered * inverse_std
    scaled_form = normal_form * gain[...]
    normed = scaled_form.astype(BF)
    normed_s[...] = normed
    kv_here[...] = dot_nt(weight[GROUP:, :], normed).astype(BF)
    for part in range(2):
        for h in range(2):
            at = pl.ds(part * GROUP + h * HDIM, HDIM)
            kv_far[mid, at, :] = kv_here[at, h * HALF : (h + 1) * HALF]

    pl.semaphore_wait(barrier, n_seq + n_dp + n_mp - 3)

    right = peer("seq", s_me, n_seq, 1)
    left = peer("seq", s_me, n_seq, -1)

    def gather_copy(way, step, piece):
        source = mid - step if way == 0 else mid + step
        target = source - 1 if way == 0 else source + 1
        at = pl.ds(piece * GROUP, GROUP)
        return remote(
            kv_far.at[source, at], kv_far.at[target, at],
            ag_ss.at[way, step, piece], ag_rs.at[way, step, piece],
            right if way == 0 else left,
        )

    steps = (mid, mid - 1)
    for piece in range(2):
        for way in range(2):
            if steps[way] > 0:
                gather_copy(way, 0, piece).start()

    for m in range(n_mp):
        to, of = pl.ds(m * LANES, GROUP), slice(m * GROUP, (m + 1) * GROUP)
        rest = pl.ds(m * LANES + GROUP, LANES - GROUP)
        mixed_pad[:, to] = scaled_form[:, of]
        mixed_pad[:, rest] = jnp.zeros((BLOCK, LANES - GROUP), F32)
        gain_pad[:, to] = gain[:, of]
        gain_pad[:, rest] = jnp.zeros((1, LANES - GROUP), F32)
    q_here[...] = dot_nt(weight[:GROUP, :], normed).astype(BF)
    go_s[...] = dot_nn(order, grad_out[...]).astype(BF)
    da_here[...] = dot_nt(out_weight[...], go_s[...]).astype(BF)
    live_key = s_me * BLOCK + position((1, BLOCK), 1) < count
    live_query = s_me * BLOCK + position((BLOCK, 1), 0) < count

    def head(h, part=0):
        return slice(part * GROUP + h * HDIM, part * GROUP + (h + 1) * HDIM)

    def far_at(h):
        return slice(h * HALF, (h + 1) * HALF)

    for h in range(2):
        q_rows[h] = dot_nt(eye, q_here[head(h), :]).astype(BF)
        da_rows[h] = dot_nt(eye, da_here[head(h), :]).astype(BF)
        near_scores[h] = jnp.where(
            live_key, dot_nn(q_rows[h], kv_here[head(h), :]) * scaling, far_below
        )
        near_probs[h] = dot_nn(da_rows[h], kv_here[head(h, 1), :])
        top[h] = jnp.maximum(
            near_scores[h, far_at(h), :HALF], near_scores[h, far_at(h), HALF:]
        )

    def far_scores(slot):
        owner = lax.rem(s_me + (slot - mid + n_seq), n_seq)
        for h in range(2):
            live = owner * BLOCK + 2 * iota((1, HALF), 1) + h < count
            score = dot_nn(q_rows[h, far_at(h), :], kv_far[slot, head(h), :]) * scaling
            score = jnp.where(live, score, far_below)
            scores[h, slot] = score
            top[h] = jnp.maximum(top[h], score)
            probs[h, slot] = dot_nn(da_rows[h, far_at(h), :], kv_far[slot, head(h, 1), :])

    place = iota((width, 1), 0).astype(F32)
    piece_at = floor_div(place, rows)
    dp_at = floor_div(piece_at, n_seq)
    feature = n_dp * rows * (piece_at - n_seq * dp_at) + rows * dp_at + (place - rows * piece_at)
    spread = one_hot(feature == iota((width, width), 1).astype(F32))

    def fill_normed():
        normed_p[...] = dot_nt(spread, normed_s[...]).astype(BF)

    def fill_go():
        go_p[...] = dot_nt(spread, go_s[...]).astype(BF)

    def fill_weight():
        for m in range(n_mp):
            weight_pad[:, m * LANES : m * LANES + GROUP] = weight[:, m * GROUP : (m + 1) * GROUP]
            weight_pad[:, m * LANES + GROUP : (m + 1) * LANES] = jnp.zeros(
                (3 * GROUP, LANES - GROUP), BF
            )

    def fill_own():
        mine = one_hot(
            (iota((width, LANES), 0) == m_me * GROUP + iota((width, LANES), 1))
            & (iota((width, LANES), 1) < GROUP)
        )
        own_parts[0] = dot_nn(go_s[...], mine)
        own_parts[1] = (dot_nn(dot_nn(order, tokens[...]).astype(BF), mine) - mean) * inverse_std
        for part in range(4):
            d_parts[part, GROUP:, :] = jnp.zeros((LANES - GROUP, BLOCK), BF)

    fillers = [fill_normed, fill_go, fill_weight, fill_own]
    far_scores(mid)
    for step in range(mid):
        for piece in range(2):
            for way in range(2):
                if step < steps[way]:
                    gather_copy(way, step, piece).wait_recv()
                    if step + 1 < steps[way]:
                        gather_copy(way, step + 1, piece).start()
        if step < len(fillers):
            fillers[step]()
        far_scores(mid - 1 - step)
        if step < steps[1]:
            far_scores(mid + 1 + step)
    for filler in fillers[mid:]:
        filler()

    inverse_total, deltas = [], []
    for h in range(2):
        far_top = jnp.max(top[h], axis=1, keepdims=True)
        total = jnp.zeros((HALF, HALF), F32)
        delta = jnp.zeros((HALF, HALF), F32)
        for slot in range(n_seq):
            grown = jnp.exp(scores[h, slot] - far_top)
            scores[h, slot] = grown
            total = total + grown
            delta = delta + grown * probs[h, slot]
        halves_total, halves_delta = [], []
        for half in range(2):
            at = far_at(half)
            near = near_scores[h, at, :]
            peak = far_top if half == h else jnp.max(near, axis=1, keepdims=True)
            grown = jnp.exp(near - peak)
            near_scores[h, at, :] = grown
            sums = row_sum(grown)
            mixed = row_sum(grown * near_probs[h, at, :])
            if half == h:
                sums = sums + row_sum(total)
                mixed = mixed + row_sum(delta)
            inverse = jnp.where(live_query[at, :], 1.0 / sums, 0.0)
            halves_total.append(inverse)
            halves_delta.append(mixed * inverse)
        inverse_total.append(halves_total)
        deltas.append(halves_delta)

    attended = [jnp.zeros((HDIM, HALF), F32) for _ in range(2)]
    d_query = [jnp.zeros((HDIM, HALF), F32) for _ in range(2)]

    def far_terms(slot):
        for h in range(2):
            weights = scores[h, slot] * inverse_total[h][h]
            bar = weights.astype(BF)
            ds = (weights * (probs[h, slot] - deltas[h][h]) * scaling).astype(BF)
            contrib[slot, head(h), :] = dot_nn(q_here[head(h), far_at(h)], ds)
            contrib[slot, head(h, 1), :] = dot_nn(da_here[head(h), far_at(h)], bar)
            attended[h] = attended[h] + dot_nt(kv_far[slot, head(h, 1), :], bar)
            d_query[h] = d_query[h] + dot_nt(kv_far[slot, head(h), :], ds)

    near_terms = []

    def near_part():
        for h in range(2):
            inverse = jnp.concatenate(inverse_total[h], axis=0)
            weights = near_scores[h] * inverse
            bar = weights.astype(BF)
            delta = jnp.concatenate(deltas[h], axis=0)
            ds = (weights * (near_probs[h] - delta) * scaling).astype(BF)
            d_key = dot_nn(q_here[head(h), :], ds)
            d_value = dot_nn(da_here[head(h), :], bar)
            near_terms.append((d_key, d_value))
            near_att = dot_nt(kv_here[head(h, 1), :], bar)
            near_dq = dot_nt(kv_here[head(h), :], ds)
            for half in range(2):
                at = far_at(half)
                att, dq = near_att[:, at], near_dq[:, at]
                if half == h:
                    att, dq = att + attended[h], dq + d_query[h]
                d_parts[0, head(h), at] = att.astype(BF)
                d_parts[1, head(h), at] = dq.astype(BF)

    def y_copy(phase, step):
        to = lax.rem(d_me + step, n_dp)
        at = pl.ds(pl.multiple_of(to * chunk, 16), chunk)
        return remote(
            y_send.at[phase, at], y_recv.at[phase, step - 1],
            y_ss.at[phase, step - 1], y_rs.at[phase, step - 1], {"dp": to},
        )

    def z_copy(phase, step):
        to = lax.rem(s_me + step, n_seq)
        at = pl.ds(pl.multiple_of(to * rows_pad, 16), rows_pad)
        return remote(
            z_send.at[phase, at], z_recv.at[phase, step - 1],
            z_ss.at[phase, step - 1], z_rs.at[phase, step - 1], {"seq": to},
        )

    def y_start(phase, sides):
        for side, (left_side, part) in enumerate(sides):
            y_send[phase, :, side * LANES : (side + 1) * LANES] = dot_nt(
                left_side[...], d_parts[part]
            ).astype(BF)
        for step in range(1, n_dp):
            y_copy(phase, step).start()

    z_order = sorted(range(1, n_seq), key=lambda step: -min(step, n_seq - step))
    widen = one_hot(
        (iota((n_seq * rows_pad, chunk), 0) // rows_pad * rows
         + iota((n_seq * rows_pad, chunk), 0) % rows_pad == iota((n_seq * rows_pad, chunk), 1))
        & (iota((n_seq * rows_pad, chunk), 0) % rows_pad < rows)
    )

    def z_start(phase):
        mine = pl.ds(pl.multiple_of(d_me * chunk, 16), chunk)
        total = y_send[phase, mine, :].astype(F32)
        for step in range(1, n_dp):
            y_copy(phase, step).wait_recv()
            total = total + y_recv[phase, step - 1].astype(F32)
        z_send[phase] = dot_nn(widen, total.astype(BF)).astype(BF)
        for step in z_order:
            z_copy(phase, step).start()

    def z_end(phase, result):
        mine = pl.ds(pl.multiple_of(s_me * rows_pad, 16), rows_pad)
        total = z_send[phase, mine, :].astype(F32)
        for step in z_order[::-1]:
            z_copy(phase, step).wait_recv()
            total = total + z_recv[phase, step - 1].astype(F32)
        result[...] = total

    def far_copy(way, step, piece):
        at = pl.ds(piece * GROUP, GROUP)
        return remote(
            far_send.at[way, step, at], far_recv.at[way, step, at],
            rs_ss.at[way, step, piece], rs_rs.at[way, step, piece],
            right if way == 0 else left,
        )

    def owner_slot(way, step):
        return (step and n_seq - step) if way == 0 else 1 + step

    todo = [owner_slot(way, step) for step in range(mid) for way in range(2) if step < steps[way]]
    todo.append(mid)
    for step in range(mid):
        for _ in range(2 if step == 0 else 4):
            if todo:
                far_terms(todo.pop(0))
        for piece in range(2):
            at = pl.ds(piece * GROUP, GROUP)
            for way in range(2):
                if step < steps[way]:
                    part = contrib[owner_slot(way, step), at, :]
                    if step > 0:
                        far_copy(way, step - 1, piece).wait_recv()
                        part = part + far_recv[way, step - 1, at, :].astype(F32)
                    far_send[way, step, at, :] = part.astype(BF)
                    far_copy(way, step, piece).start()
        if not todo and not near_terms:
            near_part()
            y_start(0, ((go_p, 0), (normed_p, 1)))
    for piece in range(2):
        at = pl.ds(piece * GROUP, GROUP)
        for way in range(2):
            if steps[way] > 0:
                far_copy(way, steps[way] - 1, piece).wait_recv()
                contrib[mid, at, :] += far_recv[way, steps[way] - 1, at, :].astype(F32)
    for h in range(2):
        for part in range(2):
            for half in range(2):
                term = near_terms[h][part][:, far_at(half)]
                if half == h:
                    term = term + contrib[mid, head(h, part), :]
                d_parts[2 + part, head(h), far_at(half)] = term.astype(BF)

    y_start(1, ((normed_p, 2), (normed_p, 3)))
    d_rows = jnp.zeros((BLOCK, n_mp * LANES), F32)
    for part in range(3):
        d_part = dot_nt(eye, d_parts[1 + part, :GROUP, :]).astype(BF)
        d_rows = d_rows + dot_nn(d_part, weight_pad[part * GROUP : (part + 1) * GROUP, :])
    d_rows = d_rows.astype(BF).astype(F32)
    first = row_sum(d_rows * gain_pad[...])
    second = row_sum(d_rows * mixed_pad[...])
    lane = iota((BLOCK, LANES), 1)
    extra = jnp.zeros((BLOCK, LANES), F32)
    for at, value in ((GROUP, first), (GROUP + 2, second)):
        coarse = value.astype(BF).astype(F32)
        extra = jnp.where(lane == at, coarse, extra)
        extra = jnp.where(lane == at + 1, value - coarse, extra)
    for m in range(n_mp):
        mp_send[m] = (d_rows[:, m * LANES : (m + 1) * LANES] + extra).astype(BF)

    def mp_copy(step):
        to = lax.rem(m_me + step, n_mp)
        return remote(
            mp_send.at[to], mp_recv.at[step - 1], mp_ss.at[step - 1], mp_rs.at[step - 1], {"mp": to}
        )

    for step in range(1, n_mp):
        mp_copy(step).start()
    z_start(0)
    z_start(1)

    d_normed = mp_send[m_me].astype(F32)
    for step in range(1, n_mp):
        mp_copy(step).wait_recv()
        d_normed = d_normed + mp_recv[step - 1].astype(F32)
    form = own_parts[1]
    gy_send[...] = jnp.broadcast_to(jnp.sum(d_normed * form, axis=0, keepdims=True), (8, LANES))

    def gy_copy(step):
        return remote(
            gy_send, gy_recv.at[step - 1], gy_ss.at[step - 1], gy_rs.at[step - 1],
            peer("dp", d_me, n_dp, step),
        )

    def gz_copy(step):
        return remote(
            gz_send, gz_recv.at[step - 1], gz_ss.at[step - 1], gz_rs.at[step - 1],
            peer("seq", s_me, n_seq, step),
        )

    for step in range(1, n_dp):
        gy_copy(step).start()
    mean_scaled = (d_normed[:, GROUP : GROUP + 1] + d_normed[:, GROUP + 1 : GROUP + 2]) * (1.0 / width)
    mean_mixed = (d_normed[:, GROUP + 2 : GROUP + 3] + d_normed[:, GROUP + 3 : GROUP + 4]) * (1.0 / width)
    scaled = d_normed * gain_pad[:, pl.ds(pl.multiple_of(m_me * LANES, LANES), LANES)]
    d_tok = own_parts[0] + (scaled - mean_scaled - form * mean_mixed) * inverse_std
    back = one_hot(iota((BLOCK, BLOCK), 0) == position((BLOCK, BLOCK), 1))
    tok_out[...] = dot_nn(back, d_tok.astype(BF)).astype(BF)[:, :GROUP]
    total = gy_send[...]
    for step in range(1, n_dp):
        gy_copy(step).wait_recv()
        total = total + gy_recv[step - 1]
    gz_send[...] = total
    for step in z_order:
        gz_copy(step).start()
    z_end(0, early_out)
    z_end(1, late_out)
    for step in z_order[::-1]:
        gz_copy(step).wait_recv()
        total = total + gz_recv[step - 1]
    gain_out[...] = total

    for way in range(2):
        for step in range(steps[way]):
            for piece in range(2):
                gather_copy(way, step, piece).wait_send()
                far_copy(way, step, piece).wait_send()
    for step in range(1, n_dp):
        for phase in range(2):
            y_copy(phase, step).wait_send()
        gy_copy(step).wait_send()
    for step in range(1, n_mp):
        mp_copy(step).wait_send()
    for step in range(1, n_seq):
        for phase in range(2):
            z_copy(phase, step).wait_send()
        gz_copy(step).wait_send()


def per_device(n_seq, n_mp, n_dp, tokens, gain, qkv_weight, out_weight, counts, grad_out):
    width = n_mp * GROUP
    chunk = width // n_dp
    rows = chunk // n_seq
    rows_pad = -(-rows // 16) * 16
    mid = n_seq // 2
    weight = qkv_weight.transpose(1, 2, 0).reshape(3 * GROUP, width)
    vmem = pl.BlockSpec(memory_space=pltpu.VMEM)
    dma = pltpu.SemaphoreType.DMA
    scratch = [
        pltpu.VMEM((n_seq, 2 * GROUP, HALF), BF),
        pltpu.VMEM((2, n_seq, HALF, HALF), F32),
        pltpu.VMEM((2, n_seq, HALF, HALF), F32),
        pltpu.VMEM((2, HALF, HALF), F32),
        pltpu.VMEM((2 * GROUP, BLOCK), BF),
        pltpu.VMEM((GROUP, BLOCK), BF),
        pltpu.VMEM((GROUP, BLOCK), BF),
        pltpu.VMEM((2, BLOCK, HDIM), BF),
        pltpu.VMEM((2, BLOCK, HDIM), BF),
        pltpu.VMEM((2, BLOCK, BLOCK), F32),
        pltpu.VMEM((2, BLOCK, BLOCK), F32),
        pltpu.VMEM((BLOCK, width), BF),
        pltpu.VMEM((BLOCK, width), BF),
        pltpu.VMEM((width, BLOCK), BF),
        pltpu.VMEM((width, BLOCK), BF),
        pltpu.VMEM((1, n_mp * LANES), F32),
        pltpu.VMEM((BLOCK, n_mp * LANES), F32),
        pltpu.VMEM((3 * GROUP, n_mp * LANES), BF),
        pltpu.VMEM((n_seq, 2 * GROUP, HALF), F32),
        pltpu.VMEM((2, mid, 2 * GROUP, HALF), BF),
        pltpu.VMEM((2, mid, 2 * GROUP, HALF), BF),
        pltpu.VMEM((4, LANES, BLOCK), BF),
        pltpu.VMEM((2, BLOCK, LANES), F32),
        pltpu.VMEM((2, width, 2 * LANES), BF),
        pltpu.VMEM((2, n_dp - 1, chunk, 2 * LANES), BF),
        pltpu.VMEM((2, n_seq * rows_pad, 2 * LANES), BF),
        pltpu.VMEM((2, n_seq - 1, rows_pad, 2 * LANES), BF),
        pltpu.VMEM((n_mp, BLOCK, LANES), BF),
        pltpu.VMEM((n_mp - 1, BLOCK, LANES), BF),
        pltpu.VMEM((8, LANES), F32),
        pltpu.VMEM((n_dp - 1, 8, LANES), F32),
        pltpu.VMEM((8, LANES), F32),
        pltpu.VMEM((n_seq - 1, 8, LANES), F32),
    ]
    for shape in (
        (2, mid, 2), (2, mid, 2), (2, n_dp - 1), (2, n_seq - 1), (n_mp - 1,), (n_dp - 1,), (n_seq - 1,),
    ):
        scratch += [dma(shape), dma(shape)]
    d_tok, early, late, d_gain = pl.pallas_call(
        functools.partial(layer_kernel, n_seq, n_mp, n_dp),
        out_shape=(
            jax.ShapeDtypeStruct((BLOCK, GROUP), BF),
            jax.ShapeDtypeStruct((rows_pad, 2 * LANES), F32),
            jax.ShapeDtypeStruct((rows_pad, 2 * LANES), F32),
            jax.ShapeDtypeStruct((8, LANES), F32),
        ),
        in_specs=[pl.BlockSpec(memory_space=pltpu.SMEM)] + [vmem] * 5,
        out_specs=(vmem,) * 4,
        scratch_shapes=scratch,
        compiler_params=pltpu.CompilerParams(
            collective_id=0, has_side_effects=True, vmem_limit_bytes=48 * 1024 * 1024
        ),
    )(counts, tokens[0], grad_out[0], gain.reshape(1, width), weight, out_weight)
    d_qkv = jnp.stack(
        [early[:rows, LANES : LANES + GROUP], late[:rows, :GROUP], late[:rows, LANES : LANES + GROUP]],
        axis=1,
    )
    return (d_tok[None], d_qkv, early[:rows, :GROUP].T, d_gain[0, :GROUP])


def solution(mesh):
    sizes = (mesh.shape["seq"], mesh.shape["mp"], mesh.shape["dp"])
    placed = (
        P("dp", "seq", None),
        P(),
        P(None, None, "mp"),
        P("mp", None),
        P("dp"),
        P("dp", "seq", None),
    )
    return jax.shard_map(
        functools.partial(per_device, *sizes),
        mesh=mesh,
        in_specs=placed,
        out_specs=(
            P("dp", "seq", "mp"),
            P(("seq", "dp"), None, "mp"),
            P("mp", ("seq", "dp")),
            P("mp"),
        ),
        check_vma=False,
    )
```

time: 524 us -> 98.9 us (0.19); the launches traced: 515 us -> 98.6 us
  waiting for transfers between devices: 287 us -> 0 us
  blocking collectives: 153 us -> 0 us
  Pallas kernels: 0 us -> 90.8 us
  local copies, waits for them, and re-layouts: 31.3 us -> 6.39 us
  matrix products: 18 us -> 0 us
  between operations: 15.8 us -> 1.32 us
  other arithmetic: 9.45 us -> 0.01 us
    unnamed x5 -> x0, waiting for transfers between devices: 208 us -> none
    psum x1 -> x0, blocking collectives: 117 us -> none  [per_device(): d_gain = lax.psum(gain_term, ('seq', 'dp'))]
    pallas_call x0 -> x1, Pallas kernels: none -> 90.8 us  [per_device(): pl.pallas_call(functools.partial(layer_kernel, n_seq, n_mp, n_dp), out_sh...]
    psum x1 -> x0, waiting for transfers between devices: 78.4 us -> none  [per_device(): lax.psum(normed_part.astype(jnp.bfloat16), 'mp').astype(jnp.float32)]
    all_gather x1 -> x0, blocking collectives: 36.3 us -> none  [per_device(): lax.all_gather(for_sending(outgoing), 'seq', axis=2, tiled=True)]
    dot_general x16 -> x0, matrix products: 16.6 us -> none  [the longest x12 11.8 us: contract(): jnp.einsum(form, left_op, right_op, preferred_element_type=jnp.float32)]
    unnamed x57 -> x12, local copies, waits for them, and re-layouts: 17.6 us -> 5.27 us
  transfers between devices with their start and end apart: 3 -> 0, of which waited for: 3 -> 0; matrix products, arithmetic and copies ran while one was open for 2% -> 0% of each run, Pallas kernels for 0% -> 0%
where the time goes in v1:
time: 98.9 us; the launch traced here: 98.6 us
  Pallas kernels  90.8 us (92%)
  local copies, waits for them, and re-layouts  6.39 us (6%)
  between operations  1.32 us (1%)
    pallas_call x1, Pallas kernels, per_device(): pl.pallas_call(functools.partial(layer_kernel, n_seq, n_mp, n_dp), out_sh...  90.8 us
    unnamed x12, local copies, waits for them, and re-layouts  5.27 us

profile of v1, /device:TPU:1, one launch (start us, length us, event | category | flops | bytes accessed | tf_op | source)
XLA Modules:
  0.0 98.6 jit_solution(11947136923070669745)
XLA Ops:
  0.6 0.0 copy-start.4
  1.3 0.0 copy-done.4
  1.3 0.0 copy-start
  1.3 1.0 %copy-done = bf16[768,3,96]{0,2,1:T(8,128)(2,1)S(1)} copy-done((bf16[768,3,96]{0,2,1:T(8,128)(2,1)S(1)}, bf16[768,3,96]{0,2,1:T(8,128)(2,1)}, u32[]{:S(2)}) %copy-start) | copy-done | bytes 442392
  2.3 0.0 copy-start.1
  2.3 1.0 %copy-done.1 = bf16[1,256,768]{2,1,0:T(8,128)(2,1)S(1)} copy-done((bf16[1,256,768]{2,1,0:T(8,128)(2,1)S(1)}, bf16[1,256,768]{2,1,0:T(8,128)(2,1)}, u32[]{:S(2)}) %copy-start.1) | copy-done | bytes 393240
  3.3 0.0 copy-start.2
  3.3 1.0 %copy-done.2 = bf16[1,256,768]{2,1,0:T(8,128)(2,1)S(1)} copy-done((bf16[1,256,768]{2,1,0:T(8,128)(2,1)S(1)}, bf16[1,256,768]{2,1,0:T(8,128)(2,1)}, u32[]{:S(2)}) %copy-start.2) | copy-done | bytes 393240
  4.3 0.0 copy-start.3
  4.3 0.9 copy-done.3
  5.2 90.8 %shard_map.93 = (bf16[256,96]{1,0:T(8,128)(2,1)S(1)}, f32[16,256]{1,0:T(8,128)S(1)}, f32[16,256]{1,0:T(8,128)S(1)}, f32[8,128]{1,0:T(8,128)S(1)}) custom-call(s32[1]{0:T(128)S(6)} %copy.12.counts, bf16[256,768]{1,0:T(8,128)(2,1)S(1)} %bitcast.17, bf16[256,768]{1,0:T(8,128)(2,1)S(1)} %bitcast.18, f32[1,768]{1,0:T(1,128)S(1)} %reshape.14.gain, ...), custom_call_target="tpu_custom_call" | custom-call | tf_op jit(solution)/shard_map/pallas_call | solution.py:501
  96.1 0.7 copy.10
  96.8 0.5 slice_bitcast_fusion.4
  97.3 0.6 slice_bitcast_fusion
  97.9 0.6 copy.11
  (3 shorter events, 0.0 us)
Async XLA Ops:
  0.6 0.7 copy-start.4
  1.3 1.0 %copy-start = (bf16[768,3,96]{0,2,1:T(8,128)(2,1)S(1)}, bf16[768,3,96]{0,2,1:T(8,128)(2,1)}, u32[]{:S(2)}) copy-start(bf16[768,3,96]{0,2,1:T(8,128)(2,1)} %param.8) | copy-start | bytes 1327108
  2.3 1.0 %copy-start.1 = (bf16[1,256,768]{2,1,0:T(8,128)(2,1)S(1)}, bf16[1,256,768]{2,1,0:T(8,128)(2,1)}, u32[]{:S(2)}) copy-start(bf16[1,256,768]{2,1,0:T(8,128)(2,1)} %param.6) | copy-start | bytes 1179652
  3.3 1.0 %copy-start.2 = (bf16[1,256,768]{2,1,0:T(8,128)(2,1)S(1)}, bf16[1,256,768]{2,1,0:T(8,128)(2,1)}, u32[]{:S(2)}) copy-start(bf16[1,256,768]{2,1,0:T(8,128)(2,1)} %param.11) | copy-start | bytes 1179652
  4.3 0.9 copy-start.3

commit v2 on v1

v2 whole, which is shorter than its diff:
```python
import functools
import math

import jax
import jax.numpy as jnp
from jax import lax
from jax.experimental import pallas as pl
from jax.experimental.pallas import tpu as pltpu
from jax.sharding import PartitionSpec as P

HDIM = 48
BLOCK = 256
HALF = BLOCK // 2
GROUP = 2 * HDIM
LANES = 128
VMEM_BYTES = 60 * 1024 * 1024
MESH = pl.DeviceIdType.MESH
BF = jnp.bfloat16
F32 = jnp.float32
far_below = -1e30


def dot_nn(left, right):
    return lax.dot_general(left, right, (((1,), (0,)), ((), ())), preferred_element_type=F32)


def dot_nt(left, right):
    return lax.dot_general(left, right, (((1,), (1,)), ((), ())), preferred_element_type=F32)


def iota(shape, axis):
    return lax.broadcasted_iota(jnp.int32, shape, axis)


def one_hot(condition):
    return jnp.where(condition, 1.0, 0.0).astype(BF)


def row_sum(value):
    return jnp.sum(value, axis=1, keepdims=True)


def floor_div(value, by):
    return jnp.floor((value + 0.5) * (1.0 / by))


def layer_kernel(
    n_seq, n_mp, n_dp,
    counts, tokens_hbm, grad_hbm, gain_hbm, weight_hbm, out_weight_hbm,
    tok_out, early_out, late_out, gain_out,
    tokens, grad_out, gain, weight, out_weight,
    kv_far, qd_far, scores, probs, scores_t, probs_t, top, kv_here, qd_here, q_rows, da_rows, k_rows, v_rows,
    near_scores, near_probs, normed_s, go_s, normed_p, go_p, gain_pad, form_pad, weight_pad,
    d_parts, own_parts, stat_send, stat_recv,
    y_send, y_recv, z_send, z_recv, mp_send, mp_recv,
    gm_send, gm_recv, gy_send, gy_recv, gz_send, gz_recv,
    in_sem, kv_ss, kv_rs, qd_ss, qd_rs, st_ss, st_rs, y_ss, y_rs, z_ss, z_rs, mp_ss, mp_rs,
    gm_ss, gm_rs, gy_ss, gy_rs, gz_ss, gz_rs,
):
    width = n_mp * GROUP
    chunk = width // n_dp
    rows = chunk // n_seq
    rows_pad = -(-rows // 16) * 16
    mid = n_seq // 2
    scaling = 1.0 / math.sqrt(HDIM)
    s_me = lax.axis_index("seq")
    m_me = lax.axis_index("mp")
    d_me = lax.axis_index("dp")
    count = counts[0]

    loads = [
        pltpu.make_async_copy(source, target, in_sem.at[at])
        for at, (source, target) in enumerate((
            (tokens_hbm, tokens), (gain_hbm, gain), (weight_hbm, weight),
            (grad_hbm, grad_out), (out_weight_hbm, out_weight),
        ))
    ]
    for load in loads:
        load.start()

    def peer(axis, me, size, step):
        return {axis: lax.rem(me + (step + size), size)}

    barrier = pltpu.get_barrier_semaphore()
    greeted = [("seq", s_me, n_seq, step) for step in sorted({2, n_seq - 2, 1, n_seq - 1})]
    greeted += [("dp", d_me, n_dp, step) for step in range(1, n_dp)]
    greeted += [("mp", m_me, n_mp, step) for step in range(1, n_mp)]
    for other in greeted:
        pl.semaphore_signal(barrier, inc=1, device_id=peer(*other), device_id_type=MESH)

    started = []

    def remote(src, dst, send, recv, device):
        return pltpu.make_async_remote_copy(
            src_ref=src, dst_ref=dst, send_sem=send, recv_sem=recv,
            device_id=device, device_id_type=MESH,
        )

    def go(copy):
        copy.start()
        started.append(copy)

    def position(shape, axis):
        at = iota(shape, axis)
        return 2 * (at % HALF) + at // HALF

    def head(h, part=0):
        return slice(part * GROUP + h * HDIM, part * GROUP + (h + 1) * HDIM)

    def far_at(h):
        return slice(h * HALF, (h + 1) * HALF)

    order = one_hot(position((BLOCK, BLOCK), 0) == iota((BLOCK, BLOCK), 1))
    eye = one_hot(iota((BLOCK, BLOCK), 0) == iota((BLOCK, BLOCK), 1))

    for load in loads[:3]:
        load.wait()
    x = dot_nn(order, tokens[...])
    mean = row_sum(x) * (1.0 / width)
    centered = x - mean
    inverse_std = lax.rsqrt(row_sum(centered * centered) * (1.0 / width) + 1e-05)
    normal_form = centered * inverse_std
    normed = (normal_form * gain[...].reshape(1, width)).astype(BF)
    normed_s[...] = normed
    kv_here[...] = dot_nt(weight[GROUP:, :], normed).astype(BF)
    for part in range(2):
        for h in range(2):
            kv_far[mid, head(h, part), :] = kv_here[head(h, part), far_at(h)]

    pl.semaphore_wait(barrier, len(greeted))

    def seq_peer(step):
        return peer("seq", s_me, n_seq, step)

    def gather_copy(which, stage, way, far, piece):
        blocks, send, recv = gathers[which]
        sign = 1 - 2 * way
        source, target = mid - sign * 2 * stage, mid - sign * (2 * stage + far)
        at = pl.ds(piece * GROUP, GROUP)
        return remote(
            blocks.at[source % n_seq, at], blocks.at[target % n_seq, at],
            send.at[stage, way, far - 1, piece], recv.at[stage, way, far - 1, piece],
            seq_peer(sign * far),
        )

    gathers = ((kv_far, kv_ss, kv_rs), (qd_far, qd_ss, qd_rs))

    def moves(stage):
        return [
            (stage, way, far, piece)
            for far in (2, 1) for piece in range(2) for way in range(2)
            if 2 * stage + far < mid or (2 * stage + far == mid and way == piece)
        ]

    def gather_stage(which, stage):
        for move in moves(stage):
            if move[2] == 2:
                gather_copy(which, *move).wait_recv()
                for later in (moves(stage + 1) if 2 * stage + 2 < mid else []):
                    if (later[1], later[3]) == (move[1], move[3]):
                        go(gather_copy(which, *later))
        for move in moves(stage):
            if move[2] == 1:
                gather_copy(which, *move).wait_recv()

    for move in moves(0):
        go(gather_copy(0, *move))
    qd_here[:GROUP, :] = dot_nt(weight[:GROUP, :], normed).astype(BF)
    for load in loads[3:]:
        load.wait()
    go_s[...] = dot_nn(order, grad_out[...]).astype(BF)
    qd_here[GROUP:, :] = dot_nt(out_weight[...], go_s[...]).astype(BF)
    for part in range(2):
        for h in range(2):
            qd_far[mid, head(h, part), :] = qd_here[head(h, part), far_at(h)]
    for move in moves(0):
        go(gather_copy(1, *move))

    live_key = s_me * BLOCK + position((1, BLOCK), 1) < count
    live_query = s_me * BLOCK + position((BLOCK, 1), 0) < count
    for h in range(2):
        q_rows[h] = dot_nt(eye, qd_here[head(h), :]).astype(BF)
        da_rows[h] = dot_nt(eye, qd_here[head(h, 1), :]).astype(BF)
        k_rows[h] = dot_nt(eye[:HALF, :HALF], kv_far[mid, head(h), :]).astype(BF)
        v_rows[h] = dot_nt(eye[:HALF, :HALF], kv_far[mid, head(h, 1), :]).astype(BF)
        near_scores[h] = jnp.where(
            live_key, dot_nn(q_rows[h], kv_here[head(h), :]) * scaling, far_below
        )
        near_probs[h] = dot_nn(da_rows[h], kv_here[head(h, 1), :])
        top[h] = jnp.maximum(
            near_scores[h, far_at(h), :HALF], near_scores[h, far_at(h), HALF:]
        )

    def far_scores(slot):
        owner = lax.rem(s_me + (slot - mid + n_seq), n_seq)
        for h in range(2):
            live = owner * BLOCK + 2 * iota((1, HALF), 1) + h < count
            score = dot_nn(q_rows[h, far_at(h), :], kv_far[slot, head(h), :]) * scaling
            score = jnp.where(live, score, far_below)
            scores[h, slot] = score
            top[h] = jnp.maximum(top[h], score)
            probs[h, slot] = dot_nn(da_rows[h, far_at(h), :], kv_far[slot, head(h, 1), :])

    def turned_scores(slot):
        for h in range(2):
            live = s_me * BLOCK + 2 * iota((HALF, 1), 0) + h < count
            score = dot_nn(k_rows[h], qd_far[slot, head(h), :]) * scaling
            scores_t[h, slot] = jnp.where(live, score, far_below)
            probs_t[h, slot] = dot_nn(v_rows[h], qd_far[slot, head(h, 1), :])

    place = iota((width, 1), 0).astype(F32)
    piece_at = floor_div(place, rows)
    dp_at = floor_div(piece_at, n_seq)
    feature = n_dp * rows * (piece_at - n_seq * dp_at) + rows * dp_at + (place - rows * piece_at)
    spread = one_hot(feature == iota((width, width), 1).astype(F32))

    def fill_pads():
        for m in range(n_mp):
            to, of = pl.ds(m * LANES, GROUP), slice(m * GROUP, (m + 1) * GROUP)
            rest = pl.ds(m * LANES + GROUP, LANES - GROUP)
            form_pad[:, to] = normal_form[:, of]
            form_pad[:, rest] = jnp.zeros((BLOCK, LANES - GROUP), F32)
            gain_pad[:, to] = gain[...].reshape(1, width)[:, of]
            gain_pad[:, rest] = jnp.zeros((1, LANES - GROUP), F32)

    def fill_normed():
        normed_p[...] = dot_nt(spread, normed_s[...]).astype(BF)

    def fill_go():
        go_p[...] = dot_nt(spread, go_s[...]).astype(BF)

    def fill_weight():
        for m in range(n_mp):
            weight_pad[:, m * LANES : m * LANES + GROUP] = weight[:, m * GROUP : (m + 1) * GROUP]
            weight_pad[:, m * LANES + GROUP : (m + 1) * LANES] = jnp.zeros(
                (3 * GROUP, LANES - GROUP), BF
            )

    def fill_own():
        mine = one_hot(
            (iota((width, LANES), 0) == m_me * GROUP + iota((width, LANES), 1))
            & (iota((width, LANES), 1) < GROUP)
        )
        own_parts[0] = dot_nn(go_s[...], mine)
        for part in range(4):
            d_parts[part, GROUP:, :] = jnp.zeros((LANES - GROUP, BLOCK), BF)

    fillers = [fill_pads, fill_normed, fill_go, fill_weight, fill_own]

    def stage_slots(stage):
        aways = (2 * stage + 1, 2 * stage + 2)
        return [mid - away for away in aways] + [mid + away for away in aways if away < mid]

    far_scores(mid)
    turned_scores(mid)
    stages = n_seq // 4
    for stage in range(stages):
        gather_stage(0, stage)
        if stage + 1 < stages:
            gather_stage(1, stage)
        for slot in stage_slots(stage):
            far_scores(slot)
        if stage + 1 < stages:
            for slot in stage_slots(stage):
                turned_scores(slot)
            for _ in range(2):
                if fillers:
                    fillers.pop(0)()
    for filler in fillers:
        filler()

    inverse_total, deltas = [], []
    lane = iota((HALF, LANES), 1)
    stats = jnp.zeros((HALF, LANES), F32)
    for h in range(2):
        far_top = jnp.max(top[h], axis=1, keepdims=True)
        total = jnp.zeros((HALF, HALF), F32)
        delta = jnp.zeros((HALF, HALF), F32)
        for slot in range(n_seq):
            grown = jnp.exp(scores[h, slot] - far_top)
            scores[h, slot] = grown
            total = total + grown
            delta = delta + grown * probs[h, slot]
        halves_total, halves_delta = [], []
        for half in range(2):
            at = far_at(half)
            near = near_scores[h, at, :]
            peak = far_top if half == h else jnp.max(near, axis=1, keepdims=True)
            grown = jnp.exp(near - peak)
            near_scores[h, at, :] = grown
            sums = row_sum(grown)
            mixed = row_sum(grown * near_probs[h, at, :])
            if half == h:
                sums = sums + row_sum(total)
                mixed = mixed + row_sum(delta)
            inverse = jnp.where(live_query[at, :], 1.0 / sums, 0.0)
            halves_total.append(inverse)
            halves_delta.append(mixed * inverse)
        inverse_total.append(halves_total)
        deltas.append(halves_delta)
        for at, value in enumerate((far_top, halves_total[h], halves_delta[h])):
            stats = jnp.where(lane == 3 * h + at, value, stats)
    stat_send[...] = jnp.transpose(stats)[:8, :]

    def stat_copy(step):
        return remote(
            stat_send, stat_recv.at[step - 1], st_ss.at[step - 1], st_rs.at[step - 1], seq_peer(step)
        )

    far_first = sorted(range(1, n_seq), key=lambda step: -min(step, n_seq - step))
    for step in far_first:
        go(stat_copy(step))

    attended = [jnp.zeros((HDIM, HALF), F32) for _ in range(2)]
    d_query = [jnp.zeros((HDIM, HALF), F32) for _ in range(2)]

    def far_terms(slot):
        for h in range(2):
            weights = scores[h, slot] * inverse_total[h][h]
            ds = (weights * (probs[h, slot] - deltas[h][h]) * scaling).astype(BF)
            attended[h] = attended[h] + dot_nt(kv_far[slot, head(h, 1), :], weights.astype(BF))
            d_query[h] = d_query[h] + dot_nt(kv_far[slot, head(h), :], ds)

    near_terms = []

    def near_part():
        for h in range(2):
            weights = near_scores[h] * jnp.concatenate(inverse_total[h], axis=0)
            bar = weights.astype(BF)
            delta = jnp.concatenate(deltas[h], axis=0)
            ds = (weights * (near_probs[h] - delta) * scaling).astype(BF)
            near_terms.append((dot_nn(qd_here[head(h), :], ds), dot_nn(qd_here[head(h, 1), :], bar)))
            near_att = dot_nt(kv_here[head(h, 1), :], bar)
            near_dq = dot_nt(kv_here[head(h), :], ds)
            for half in range(2):
                at = far_at(half)
                att, dq = near_att[:, at], near_dq[:, at]
                if half == h:
                    att, dq = att + attended[h], dq + d_query[h]
                d_parts[0, head(h), at] = att.astype(BF)
                d_parts[1, head(h), at] = dq.astype(BF)

    def y_copy(phase, step):
        to = lax.rem(d_me + step, n_dp)
        at = pl.ds(pl.multiple_of(to * chunk, 16), chunk)
        return remote(
            y_send.at[phase, at], y_recv.at[phase, step - 1],
            y_ss.at[phase, step - 1], y_rs.at[phase, step - 1], {"dp": to},
        )

    def z_copy(phase, step):
        to = lax.rem(s_me + step, n_seq)
        at = pl.ds(pl.multiple_of(to * rows_pad, 16), rows_pad)
        return remote(
            z_send.at[phase, at], z_recv.at[phase, step - 1],
            z_ss.at[phase, step - 1], z_rs.at[phase, step - 1], {"seq": to},
        )

    def y_start(phase, sides):
        for side, (left_side, part) in enumerate(sides):
            y_send[phase, :, side * LANES : (side + 1) * LANES] = dot_nt(
                left_side[...], d_parts[part]
            ).astype(BF)
        for step in range(1, n_dp):
            go(y_copy(phase, step))

    widen = one_hot(
        (iota((n_seq * rows_pad, chunk), 0) // rows_pad * rows
         + iota((n_seq * rows_pad, chunk), 0) % rows_pad == iota((n_seq * rows_pad, chunk), 1))
        & (iota((n_seq * rows_pad, chunk), 0) % rows_pad < rows)
    )

    def z_start(phase):
        mine = pl.ds(pl.multiple_of(d_me * chunk, 16), chunk)
        total = y_send[phase, mine, :].astype(F32)
        for step in range(1, n_dp):
            y_copy(phase, step).wait_recv()
            total = total + y_recv[phase, step - 1].astype(F32)
        z_send[phase] = dot_nn(widen, total.astype(BF)).astype(BF)
        for step in far_first:
            go(z_copy(phase, step))

    def z_end(phase, result):
        mine = pl.ds(pl.multiple_of(s_me * rows_pad, 16), rows_pad)
        total = z_send[phase, mine, :].astype(F32)
        for step in far_first[::-1]:
            z_copy(phase, step).wait_recv()
            total = total + z_recv[phase, step - 1].astype(F32)
        result[...] = total

    for slot in range(n_seq):
        far_terms(slot)
    near_part()
    y_start(0, ((go_p, 0), (normed_p, 1)))
    gather_stage(1, stages - 1)
    for slot in stage_slots(stages - 1):
        turned_scores(slot)

    far_dk = [jnp.zeros((HDIM, HALF), F32) for _ in range(2)]
    far_dv = [jnp.zeros((HDIM, HALF), F32) for _ in range(2)]

    def key_terms(slot, stat):
        for h in range(2):
            weights = jnp.exp(scores_t[h, slot] - stat[3 * h : 3 * h + 1, :]) * stat[3 * h + 1 : 3 * h + 2, :]
            ds = (weights * (probs_t[h, slot] - stat[3 * h + 2 : 3 * h + 3, :]) * scaling).astype(BF)
            far_dk[h] = far_dk[h] + dot_nt(qd_far[slot, head(h), :], ds)
            far_dv[h] = far_dv[h] + dot_nt(qd_far[slot, head(h, 1), :], weights.astype(BF))

    key_terms(mid, stat_send[...])
    near_first = far_first[::-1]
    for at, step in enumerate(near_first):
        if at == len(near_first) // 2:
            z_start(0)
        stat_copy(step).wait_recv()
        key_terms((mid - step) % n_seq, stat_recv[step - 1])
    for h in range(2):
        for part, far_part in ((0, far_dk), (1, far_dv)):
            for half in range(2):
                term = near_terms[h][part][:, far_at(half)]
                if half == h:
                    term = term + far_part[h]
                d_parts[2 + part, head(h), far_at(half)] = term.astype(BF)

    y_start(1, ((normed_p, 2), (normed_p, 3)))
    d_rows = jnp.zeros((BLOCK, n_mp * LANES), F32)
    for part in range(3):
        d_part = dot_nt(eye, d_parts[1 + part, :GROUP, :]).astype(BF)
        d_rows = d_rows + dot_nn(d_part, weight_pad[part * GROUP : (part + 1) * GROUP, :])
    d_rows = d_rows.astype(BF).astype(F32)
    gain_terms = jnp.sum(d_rows * form_pad[...], axis=0, keepdims=True)
    for m in range(n_mp):
        gm_send[m] = jnp.broadcast_to(gain_terms[:, m * LANES : (m + 1) * LANES], (8, LANES))

    def gm_copy(step):
        to = lax.rem(m_me + step, n_mp)
        return remote(
            gm_send.at[to], gm_recv.at[step - 1], gm_ss.at[step - 1], gm_rs.at[step - 1], {"mp": to}
        )

    def gy_copy(step):
        return remote(
            gy_send, gy_recv.at[step - 1], gy_ss.at[step - 1], gy_rs.at[step - 1],
            peer("dp", d_me, n_dp, step),
        )

    def gz_copy(step):
        return remote(
            gz_send, gz_recv.at[step - 1], gz_ss.at[step - 1], gz_rs.at[step - 1], seq_peer(step)
        )

    for step in range(1, n_mp):
        go(gm_copy(step))
    scaled_rows = d_rows * gain_pad[...]
    first = row_sum(scaled_rows)
    second = row_sum(scaled_rows * form_pad[...])
    lane = iota((BLOCK, LANES), 1)
    extra = jnp.zeros((BLOCK, LANES), F32)
    for at, value in ((GROUP, first), (GROUP + 2, second)):
        coarse = value.astype(BF).astype(F32)
        extra = jnp.where(lane == at, coarse, extra)
        extra = jnp.where(lane == at + 1, value - coarse, extra)
    for m in range(n_mp):
        mp_send[m] = (d_rows[:, m * LANES : (m + 1) * LANES] + extra).astype(BF)

    def mp_copy(step):
        to = lax.rem(m_me + step, n_mp)
        return remote(
            mp_send.at[to], mp_recv.at[step - 1], mp_ss.at[step - 1], mp_rs.at[step - 1], {"mp": to}
        )

    for step in range(1, n_mp):
        go(mp_copy(step))
    gain_total = gm_send[m_me]
    for step in range(1, n_mp):
        gm_copy(step).wait_recv()
        gain_total = gain_total + gm_recv[step - 1]
    gy_send[...] = gain_total
    for step in range(1, n_dp):
        go(gy_copy(step))
    z_start(1)
    for step in range(1, n_dp):
        gy_copy(step).wait_recv()
        gain_total = gain_total + gy_recv[step - 1]
    gz_send[...] = gain_total
    for step in far_first:
        go(gz_copy(step))

    d_normed = mp_send[m_me].astype(F32)
    for step in range(1, n_mp):
        mp_copy(step).wait_recv()
        d_normed = d_normed + mp_recv[step - 1].astype(F32)
    own = pl.ds(pl.multiple_of(m_me * LANES, LANES), LANES)
    form = form_pad[:, own]
    mean_scaled = (d_normed[:, GROUP : GROUP + 1] + d_normed[:, GROUP + 1 : GROUP + 2]) * (1.0 / width)
    mean_mixed = (d_normed[:, GROUP + 2 : GROUP + 3] + d_normed[:, GROUP + 3 : GROUP + 4]) * (1.0 / width)
    scaled = d_normed * gain_pad[:, own]
    d_tok = own_parts[0] + (scaled - mean_scaled - form * mean_mixed) * inverse_std
    turned = dot_nt(eye[:LANES, :LANES], d_tok.astype(BF)).astype(BF)
    tok_out[...] = dot_nn(turned, order).astype(BF)[:GROUP, :]
    z_end(0, early_out)
    z_end(1, late_out)
    for step in far_first[::-1]:
        gz_copy(step).wait_recv()
        gain_total = gain_total + gz_recv[step - 1]
    gain_out[...] = gain_total
    for copy in started:
        copy.wait_send()


def per_device(n_seq, n_mp, n_dp, tokens, gain, qkv_weight, out_weight, counts, grad_out):
    width = n_mp * GROUP
    chunk = width // n_dp
    rows = chunk // n_seq
    rows_pad = -(-rows // 16) * 16
    mid = n_seq // 2
    weight = qkv_weight.transpose(1, 2, 0).reshape(3 * GROUP, width)
    vmem = pl.BlockSpec(memory_space=pltpu.VMEM)
    dma = pltpu.SemaphoreType.DMA
    far_block = pltpu.VMEM((n_seq, 2 * GROUP, HALF), BF)
    far_square = pltpu.VMEM((2, n_seq, HALF, HALF), F32)
    scratch = [
        pltpu.VMEM((BLOCK, width), BF),
        pltpu.VMEM((BLOCK, width), BF),
        pltpu.VMEM((width,), F32),
        pltpu.VMEM((3 * GROUP, width), BF),
        pltpu.VMEM((GROUP, width), BF),
        far_block, far_block, far_square, far_square, far_square, far_square,
        pltpu.VMEM((2, HALF, HALF), F32),
        pltpu.VMEM((2 * GROUP, BLOCK), BF),
        pltpu.VMEM((2 * GROUP, BLOCK), BF),
        pltpu.VMEM((2, BLOCK, HDIM), BF),
        pltpu.VMEM((2, BLOCK, HDIM), BF),
        pltpu.VMEM((2, HALF, HDIM), BF),
        pltpu.VMEM((2, HALF, HDIM), BF),
        pltpu.VMEM((2, BLOCK, BLOCK), F32),
        pltpu.VMEM((2, BLOCK, BLOCK), F32),
        pltpu.VMEM((BLOCK, width), BF),
        pltpu.VMEM((BLOCK, width), BF),
        pltpu.VMEM((width, BLOCK), BF),
        pltpu.VMEM((width, BLOCK), BF),
        pltpu.VMEM((1, n_mp * LANES), F32),
        pltpu.VMEM((BLOCK, n_mp * LANES), F32),
        pltpu.VMEM((3 * GROUP, n_mp * LANES), BF),
        pltpu.VMEM((4, LANES, BLOCK), BF),
        pltpu.VMEM((1, BLOCK, LANES), F32),
        pltpu.VMEM((8, LANES), F32),
        pltpu.VMEM((n_seq - 1, 8, LANES), F32),
        pltpu.VMEM((2, width, 2 * LANES), BF),
        pltpu.VMEM((2, n_dp - 1, chunk, 2 * LANES), BF),
        pltpu.VMEM((2, n_seq * rows_pad, 2 * LANES), BF),
        pltpu.VMEM((2, n_seq - 1, rows_pad, 2 * LANES), BF),
        pltpu.VMEM((n_mp, BLOCK, LANES), BF),
        pltpu.VMEM((n_mp - 1, BLOCK, LANES), BF),
        pltpu.VMEM((n_mp, 8, LANES), F32),
        pltpu.VMEM((n_mp - 1, 8, LANES), F32),
        pltpu.VMEM((8, LANES), F32),
        pltpu.VMEM((n_dp - 1, 8, LANES), F32),
        pltpu.VMEM((8, LANES), F32),
        pltpu.VMEM((n_seq - 1, 8, LANES), F32),
        dma((5,)),
    ]
    for shape in (
        (n_seq // 4, 2, 2, 2), (n_seq // 4, 2, 2, 2), (n_seq - 1,), (2, n_dp - 1), (2, n_seq - 1), (n_mp - 1,),
        (n_mp - 1,), (n_dp - 1,), (n_seq - 1,),
    ):
        scratch += [dma(shape), dma(shape)]
    d_tok, early, late, d_gain = pl.pallas_call(
        functools.partial(layer_kernel, n_seq, n_mp, n_dp),
        out_shape=(
            jax.ShapeDtypeStruct((GROUP, BLOCK), BF),
            jax.ShapeDtypeStruct((rows_pad, 2 * LANES), F32),
            jax.ShapeDtypeStruct((rows_pad, 2 * LANES), F32),
            jax.ShapeDtypeStruct((8, LANES), F32),
        ),
        in_specs=[pl.BlockSpec(memory_space=pltpu.SMEM)] + [pl.BlockSpec(memory_space=pl.ANY)] * 5,
        out_specs=(vmem,) * 4,
        scratch_shapes=scratch,
        compiler_params=pltpu.CompilerParams(
            collective_id=0, has_side_effects=True, vmem_limit_bytes=VMEM_BYTES
        ),
    )(counts, tokens[0], grad_out[0], gain, weight, out_weight)
    tok_turned, d_qkv, out_turned, gain_total = pl.pallas_call(
        functools.partial(shape_results, rows),
        out_shape=(
            jax.ShapeDtypeStruct((GROUP, BLOCK), BF),
            jax.ShapeDtypeStruct((rows, 3, GROUP), F32),
            jax.ShapeDtypeStruct((rows, GROUP), F32),
            jax.ShapeDtypeStruct((GROUP,), F32),
        ),
        in_specs=[vmem] * 4,
        out_specs=(vmem,) * 4,
        compiler_params=pltpu.CompilerParams(vmem_limit_bytes=VMEM_BYTES),
    )(d_tok, early, late, d_gain)
    return (tok_turned.T[None], d_qkv, out_turned.T, gain_total)


def shape_results(rows, d_tok, early, late, d_gain, tok_out, qkv_out, out_out, gain_out):
    tok_out[...] = d_tok[...]
    qkv_out[:, 0, :] = early[:rows, LANES : LANES + GROUP]
    qkv_out[:, 1, :] = late[:rows, :GROUP]
    qkv_out[:, 2, :] = late[:rows, LANES : LANES + GROUP]
    out_out[...] = early[:rows, :GROUP]
    gain_out[...] = d_gain[0, :GROUP]


def solution(mesh):
    sizes = (mesh.shape["seq"], mesh.shape["mp"], mesh.shape["dp"])
    placed = (
        P("dp", "seq", None),
        P(),
        P(None, None, "mp"),
        P("mp", None),
        P("dp"),
        P("dp", "seq", None),
    )
    return jax.shard_map(
        functools.partial(per_device, *sizes),
        mesh=mesh,
        in_specs=placed,
        out_specs=(
            P("dp", "seq", "mp"),
            P(("seq", "dp"), None, "mp"),
            P("mp", ("seq", "dp")),
            P("mp"),
        ),
        check_vma=False,
    )
```

time: 98.9 us -> 71.7 us (0.72)
  Pallas kernels: 90.8 us -> 70.2 us
  local copies, waits for them, and re-layouts: 6.39 us -> 0 us
    pallas_call x1, Pallas kernels: 90.8 us -> 68.8 us  [per_device(): pl.pallas_call(functools.partial(layer_kernel, n_seq, n_mp, n_dp), out_sh...]
    unnamed x12 -> x0, local copies, waits for them, and re-layouts: 5.27 us -> none
    pallas_call x0 -> x1, Pallas kernels: none -> 1.46 us  [per_device(): pl.pallas_call(functools.partial(shape_results, rows), out_shape=(jax.Sha...]
where the time goes in v2:
time: 71.7 us; the launch traced here: 71.5 us
  Pallas kernels  70.2 us (98%)
  between operations  1.29 us (2%)
    pallas_call x1, Pallas kernels, per_device(): pl.pallas_call(functools.partial(layer_kernel, n_seq, n_mp, n_dp), out_sh...  68.8 us
    pallas_call x1, Pallas kernels, per_device(): pl.pallas_call(functools.partial(shape_results, rows), out_shape=(jax.Sha...  1.46 us

profile of v2, /device:TPU:1, one launch (start us, length us, event | category | flops | bytes accessed | tf_op | source)
XLA Modules:
  0.0 71.5 jit_solution(6655526216204606182)
XLA Ops:
  1.3 68.8 %shard_map.93 = (bf16[96,256]{1,0:T(8,128)(2,1)}, f32[16,256]{1,0:T(8,128)}, f32[16,256]{1,0:T(8,128)}, f32[8,128]{1,0:T(8,128)}) custom-call(s32[1]{0:T(128)S(6)} %copy.10.counts, bf16[256,768]{1,0:T(8,128)(2,1)} %bitcast.10, bf16[256,768]{1,0:T(8,128)(2,1)} %bitcast.11, f32[768]{0:T(1024)} %gain_hbm.1, bf16[288,768]{1,0:T(8,128)(2,1)} %bitcast.9, ...), custom_call_target="tpu_custom_call" | custom-call | tf_op jit(solution)/shard_map/pallas_call | solution.py:567
  70.0 1.5 %shard_map.94 = (bf16[96,256]{1,0:T(8,128)(2,1)}, f32[12,3,96]{2,1,0:T(4,128)}, f32[12,96]{1,0:T(8,128)}, f32[96]{0:T(128)}) custom-call(bf16[96,256]{1,0:T(8,128)(2,1)} %get-tuple-element.12.d_tok, f32[16,256]{1,0:T(8,128)} %get-tuple-element.13.early, f32[16,256]{1,0:T(8,128)} %get-tuple-element.14.late, f32[8,128]{1,0:T(8,128)} %get-tuple-element.15.d_gain), custom_call_target="tpu_custom_call" | custom-call | tf_op jit(solution)/shard_map/pallas_call | solution.py:582

commit v3 on v2

--- a/solution.py
+++ b/solution.py
@@ -47,15 +47,15 @@
 def layer_kernel(
     n_seq, n_mp, n_dp,
     counts, tokens_hbm, grad_hbm, gain_hbm, weight_hbm, out_weight_hbm,
-    tok_out, early_out, late_out, gain_out,
+    tok_out, qkv_out, out_out, gain_out,
     tokens, grad_out, gain, weight, out_weight,
     kv_far, qd_far, scores, probs, scores_t, probs_t, top, kv_here, qd_here, q_rows, da_rows, k_rows, v_rows,
     near_scores, near_probs, normed_s, go_s, normed_p, go_p, gain_pad, form_pad, weight_pad,
     d_parts, own_parts, stat_send, stat_recv,
-    y_send, y_recv, z_send, z_recv, mp_send, mp_recv,
-    gm_send, gm_recv, gy_send, gy_recv, gz_send, gz_recv,
-    in_sem, kv_ss, kv_rs, qd_ss, qd_rs, st_ss, st_rs, y_ss, y_rs, z_ss, z_rs, mp_ss, mp_rs,
-    gm_ss, gm_rs, gy_ss, gy_rs, gz_ss, gz_rs,
+    side_recv, y_recv, z_send, z_recv, mp_send, mp_recv,
+    gm_send, gm_recv, gy_send, gy_recv,
+    in_sem, kv_ss, kv_rs, qd_ss, qd_rs, st_ss, st_rs, sd_ss, sd_rs, y_ss, y_rs, z_ss, z_rs, mp_ss, mp_rs,
+    gm_ss, gm_rs, gy_ss, gy_rs,
 ):
     width = n_mp * GROUP
     chunk = width // n_dp
@@ -113,15 +113,16 @@
     order = one_hot(position((BLOCK, BLOCK), 0) == iota((BLOCK, BLOCK), 1))
     eye = one_hot(iota((BLOCK, BLOCK), 0) == iota((BLOCK, BLOCK), 1))
 
-    for load in loads[:3]:
-        load.wait()
+    loads[0].wait()
     x = dot_nn(order, tokens[...])
     mean = row_sum(x) * (1.0 / width)
     centered = x - mean
     inverse_std = lax.rsqrt(row_sum(centered * centered) * (1.0 / width) + 1e-05)
     normal_form = centered * inverse_std
+    loads[1].wait()
     normed = (normal_form * gain[...].reshape(1, width)).astype(BF)
     normed_s[...] = normed
+    loads[2].wait()
     kv_here[...] = dot_nt(weight[GROUP:, :], normed).astype(BF)
     for part in range(2):
         for h in range(2):
@@ -223,11 +224,25 @@
             gain_pad[:, to] = gain[...].reshape(1, width)[:, of]
             gain_pad[:, rest] = jnp.zeros((1, LANES - GROUP), F32)
 
+    def chunk_of(device):
+        return pl.ds(pl.multiple_of(device * chunk, 16), chunk)
+
+    def side_copy(side, step):
+        to = lax.rem(d_me + step, n_dp)
+        return remote(
+            (go_p, normed_p)[side].at[chunk_of(to)], side_recv.at[side, step - 1],
+            sd_ss.at[side, step - 1], sd_rs.at[side, step - 1], {"dp": to},
+        )
+
     def fill_normed():
         normed_p[...] = dot_nt(spread, normed_s[...]).astype(BF)
+        for step in range(1, n_dp):
+            go(side_copy(1, step))
 
     def fill_go():
         go_p[...] = dot_nt(spread, go_s[...]).astype(BF)
+        for step in range(1, n_dp):
+            go(side_copy(0, step))
 
     def fill_weight():
         for m in range(n_mp):
@@ -242,8 +257,7 @@
             & (iota((width, LANES), 1) < GROUP)
         )
         own_parts[0] = dot_nn(go_s[...], mine)
-        for part in range(4):
-            d_parts[part, GROUP:, :] = jnp.zeros((LANES - GROUP, BLOCK), BF)
+        z_send[...] = jnp.zeros(z_send.shape, BF)
 
     fillers = [fill_pads, fill_normed, fill_go, fill_weight, fill_own]
 
@@ -254,51 +268,75 @@
     far_scores(mid)
     turned_scores(mid)
     stages = n_seq // 4
-    for stage in range(stages):
+    lag = min(1, stages - 1)
+    done = [mid]
+    for stage in range(stages - 1):
         gather_stage(0, stage)
-        if stage + 1 < stages:
-            gather_stage(1, stage)
+        if stage >= lag:
+            gather_stage(1, stage - lag)
         for slot in stage_slots(stage):
             far_scores(slot)
-        if stage + 1 < stages:
-            for slot in stage_slots(stage):
+            done.append(slot)
+        if stage >= lag:
+            for slot in stage_slots(stage - lag):
                 turned_scores(slot)
-            for _ in range(2):
-                if fillers:
-                    fillers.pop(0)()
+        for _ in range(2):
+            if fillers:
+                fillers.pop(0)()
     for filler in fillers:
         filler()
 
-    inverse_total, deltas = [], []
+    def grow(h, slots, peak):
+        total = jnp.zeros((HALF, HALF), F32)
+        delta = jnp.zeros((HALF, HALF), F32)
+        for slot in slots:
+            grown = jnp.exp(scores[h, slot] - peak)
+            scores[h, slot] = grown
+            total = total + grown
+            delta = delta + grown * probs[h, slot]
+        return row_sum(total), row_sum(delta)
+
+    first_peaks, first_sums = [], []
+    for h in range(2):
+        peaks, sums = [], []
+        for half in range(2):
+            at = far_at(half)
+            near = near_scores[h, at, :]
+            peak = jnp.max(top[h] if half == h else near, axis=1, keepdims=True)
+            grown = jnp.exp(near - peak)
+            near_scores[h, at, :] = grown
+            total, delta = row_sum(grown), row_sum(grown * near_probs[h, at, :])
+            if half == h:
+                far_total, far_delta = grow(h, done, peak)
+                total, delta = total + far_total, delta + far_delta
+            peaks.append(peak)
+            sums.append((total, delta))
+        first_peaks.append(peaks)
+        first_sums.append(sums)
+
+    gather_stage(0, stages - 1)
+    last = stage_slots(stages - 1)
+    for slot in last:
+        far_scores(slot)
+    inverse_total, inverse_first, deltas = [], [], []
     lane = iota((HALF, LANES), 1)
     stats = jnp.zeros((HALF, LANES), F32)
     for h in range(2):
         far_top = jnp.max(top[h], axis=1, keepdims=True)
-        total = jnp.zeros((HALF, HALF), F32)
-        delta = jnp.zeros((HALF, HALF), F32)
-        for slot in range(n_seq):
-            grown = jnp.exp(scores[h, slot] - far_top)
-            scores[h, slot] = grown
-            total = total + grown
-            delta = delta + grown * probs[h, slot]
-        halves_total, halves_delta = [], []
-        for half in range(2):
-            at = far_at(half)
-            near = near_scores[h, at, :]
-            peak = far_top if half == h else jnp.max(near, axis=1, keepdims=True)
-            grown = jnp.exp(near - peak)
-            near_scores[h, at, :] = grown
-            sums = row_sum(grown)
-            mixed = row_sum(grown * near_probs[h, at, :])
-            if half == h:
-                sums = sums + row_sum(total)
-                mixed = mixed + row_sum(delta)
-            inverse = jnp.where(live_query[at, :], 1.0 / sums, 0.0)
-            halves_total.append(inverse)
-            halves_delta.append(mixed * inverse)
-        inverse_total.append(halves_total)
-        deltas.append(halves_delta)
-        for at, value in enumerate((far_top, halves_total[h], halves_delta[h])):
+        shrink = jnp.exp(first_peaks[h][h] - far_top)
+        last_total, last_delta = grow(h, last, far_top)
+        total, delta = first_sums[h][h]
+        inverse = jnp.where(
+            live_query[far_at(h), :], 1.0 / (total * shrink + last_total), 0.0
+        )
+        far_delta = (delta * shrink + last_delta) * inverse
+        total, delta = first_sums[h][1 - h]
+        other = jnp.where(live_query[far_at(1 - h), :], 1.0 / total, 0.0)
+        pairs = [(shrink * inverse, far_delta), (other, delta * other)]
+        inverse_total.append(inverse)
+        inverse_first.append([pairs[half != h][0] for half in range(2)])
+        deltas.append([pairs[half != h][1] for half in range(2)])
+        for at, value in enumerate((far_top, inverse, far_delta)):
             stats = jnp.where(lane == 3 * h + at, value, stats)
     stat_send[...] = jnp.transpose(stats)[:8, :]
 
@@ -316,7 +354,7 @@
 
     def far_terms(slot):
         for h in range(2):
-            weights = scores[h, slot] * inverse_total[h][h]
+            weights = scores[h, slot] * (inverse_total[h] if slot in last else inverse_first[h][h])
             ds = (weights * (probs[h, slot] - deltas[h][h]) * scaling).astype(BF)
             attended[h] = attended[h] + dot_nt(kv_far[slot, head(h, 1), :], weights.astype(BF))
             d_query[h] = d_query[h] + dot_nt(kv_far[slot, head(h), :], ds)
@@ -325,7 +363,7 @@
 
     def near_part():
         for h in range(2):
-            weights = near_scores[h] * jnp.concatenate(inverse_total[h], axis=0)
+            weights = near_scores[h] * jnp.concatenate(inverse_first[h], axis=0)
             bar = weights.astype(BF)
             delta = jnp.concatenate(deltas[h], axis=0)
             ds = (weights * (near_probs[h] - delta) * scaling).astype(BF)
@@ -341,11 +379,9 @@
                 d_parts[1, head(h), at] = dq.astype(BF)
 
     def y_copy(phase, step):
-        to = lax.rem(d_me + step, n_dp)
-        at = pl.ds(pl.multiple_of(to * chunk, 16), chunk)
-        return remote(
-            y_send.at[phase, at], y_recv.at[phase, step - 1],
-            y_ss.at[phase, step - 1], y_rs.at[phase, step - 1], {"dp": to},
+        return remote(
+            d_parts.at[pl.ds(2 * phase, 2)], y_recv.at[phase, step - 1],
+            y_ss.at[phase, step - 1], y_rs.at[phase, step - 1], peer("dp", d_me, n_dp, step),
         )
 
     def z_copy(phase, step):
@@ -356,11 +392,7 @@
             z_ss.at[phase, step - 1], z_rs.at[phase, step - 1], {"seq": to},
         )
 
-    def y_start(phase, sides):
-        for side, (left_side, part) in enumerate(sides):
-            y_send[phase, :, side * LANES : (side + 1) * LANES] = dot_nt(
-                left_side[...], d_parts[part]
-            ).astype(BF)
+    def y_start(phase):
         for step in range(1, n_dp):
             go(y_copy(phase, step))
 
@@ -371,30 +403,51 @@
     )
 
     def z_start(phase):
-        mine = pl.ds(pl.multiple_of(d_me * chunk, 16), chunk)
-        total = y_send[phase, mine, :].astype(F32)
+        mine = chunk_of(d_me)
+        sides = ((go_p, 0), (normed_p, 1)) if phase == 0 else ((normed_p, 1), (normed_p, 1))
+        if phase == 0:
+            for side in range(2):
+                for step in range(1, n_dp):
+                    side_copy(side, step).wait_recv()
+        sums = [dot_nt(side[mine, :], d_parts[2 * phase + at]) for at, (side, _) in enumerate(sides)]
         for step in range(1, n_dp):
             y_copy(phase, step).wait_recv()
-            total = total + y_recv[phase, step - 1].astype(F32)
-        z_send[phase] = dot_nn(widen, total.astype(BF)).astype(BF)
+            for at, (_, side) in enumerate(sides):
+                sums[at] = sums[at] + dot_nt(side_recv[side, step - 1], y_recv[phase, step - 1, at])
+        for at in range(2):
+            z_send[phase, :, at * LANES : at * LANES + GROUP] = dot_nn(
+                widen, sums[at].astype(BF)
+            ).astype(BF)
+
+    def z_go(phase):
         for step in far_first:
             go(z_copy(phase, step))
 
-    def z_end(phase, result):
+    def z_end(phase):
         mine = pl.ds(pl.multiple_of(s_me * rows_pad, 16), rows_pad)
         total = z_send[phase, mine, :].astype(F32)
         for step in far_first[::-1]:
             z_copy(phase, step).wait_recv()
             total = total + z_recv[phase, step - 1].astype(F32)
-        result[...] = total
-
-    for slot in range(n_seq):
+        return total
+
+    waiting = list(range(stages - 1 - lag, stages))
+    if stages > 1:
+        gather_stage(1, waiting[0])
+    for slot in done:
+        far_terms(slot)
+    if stages > 1:
+        for slot in stage_slots(waiting.pop(0)):
+            turned_scores(slot)
+    for stage in waiting:
+        gather_stage(1, stage)
+    for slot in last:
         far_terms(slot)
     near_part()
-    y_start(0, ((go_p, 0), (normed_p, 1)))
-    gather_stage(1, stages - 1)
-    for slot in stage_slots(stages - 1):
-        turned_scores(slot)
+    y_start(0)
+    for stage in waiting:
+        for slot in stage_slots(stage):
+            turned_scores(slot)
 
     far_dk = [jnp.zeros((HDIM, HALF), F32) for _ in range(2)]
     far_dv = [jnp.zeros((HDIM, HALF), F32) for _ in range(2)]
@@ -408,9 +461,7 @@
 
     key_terms(mid, stat_send[...])
     near_first = far_first[::-1]
-    for at, step in enumerate(near_first):
-        if at == len(near_first) // 2:
-            z_start(0)
+    for step in near_first:
         stat_copy(step).wait_recv()
         key_terms((mid - step) % n_seq, stat_recv[step - 1])
     for h in range(2):
@@ -421,15 +472,15 @@
                     term = term + far_part[h]
                 d_parts[2 + part, head(h), far_at(half)] = term.astype(BF)
 
-    y_start(1, ((normed_p, 2), (normed_p, 3)))
+    y_start(1)
     d_rows = jnp.zeros((BLOCK, n_mp * LANES), F32)
     for part in range(3):
-        d_part = dot_nt(eye, d_parts[1 + part, :GROUP, :]).astype(BF)
+        d_part = dot_nt(eye, d_parts[1 + part]).astype(BF)
         d_rows = d_rows + dot_nn(d_part, weight_pad[part * GROUP : (part + 1) * GROUP, :])
     d_rows = d_rows.astype(BF).astype(F32)
     gain_terms = jnp.sum(d_rows * form_pad[...], axis=0, keepdims=True)
     for m in range(n_mp):
-        gm_send[m] = jnp.broadcast_to(gain_terms[:, m * LANES : (m + 1) * LANES], (8, LANES))
+        gm_send[m] = gain_terms[:, m * LANES : (m + 1) * LANES]
 
     def gm_copy(step):
         to = lax.rem(m_me + step, n_mp)
@@ -443,13 +494,10 @@
             peer("dp", d_me, n_dp, step),
         )
 
-    def gz_copy(step):
-        return remote(
-            gz_send, gz_recv.at[step - 1], gz_ss.at[step - 1], gz_rs.at[step - 1], seq_peer(step)
-        )
-
     for step in range(1, n_mp):
         go(gm_copy(step))
+    z_start(0)
+    z_go(0)
     scaled_rows = d_rows * gain_pad[...]
     first = row_sum(scaled_rows)
     second = row_sum(scaled_rows * form_pad[...])
@@ -481,9 +529,14 @@
     for step in range(1, n_dp):
         gy_copy(step).wait_recv()
         gain_total = gain_total + gy_recv[step - 1]
-    gz_send[...] = gain_total
-    for step in far_first:
-        go(gz_copy(step))
+    coarse = gain_total.astype(BF).astype(F32)
+    spare = iota((n_seq * rows_pad, LANES), 0) % rows_pad == rows
+    for at, value in enumerate((coarse, gain_total - coarse)):
+        lanes_at = slice(at * LANES, (at + 1) * LANES)
+        z_send[1, :, lanes_at] = jnp.where(
+            spare, value, z_send[1, :, lanes_at].astype(F32)
+        ).astype(BF)
+    z_go(1)
 
     d_normed = mp_send[m_me].astype(F32)
     for step in range(1, n_mp):
@@ -497,13 +550,16 @@
     d_tok = own_parts[0] + (scaled - mean_scaled - form * mean_mixed) * inverse_std
     turned = dot_nt(eye[:LANES, :LANES], d_tok.astype(BF)).astype(BF)
     tok_out[...] = dot_nn(turned, order).astype(BF)[:GROUP, :]
-    z_end(0, early_out)
-    z_end(1, late_out)
-    for step in far_first[::-1]:
-        gz_copy(step).wait_recv()
-        gain_total = gain_total + gz_recv[step - 1]
-    gain_out[...] = gain_total
-    for copy in started:
+    for copy in started[: 1 - n_seq]:
+        copy.wait_send()
+    early = z_end(0)
+    qkv_out[:, 0, :] = early[:rows, LANES : LANES + GROUP]
+    out_out[...] = early[:rows, :GROUP]
+    late = z_end(1)
+    qkv_out[:, 1, :] = late[:rows, :GROUP]
+    qkv_out[:, 2, :] = late[:rows, LANES : LANES + GROUP]
+    gain_out[...] = late[rows : rows + 1, :GROUP] + late[rows : rows + 1, LANES : LANES + GROUP]
+    for copy in started[1 - n_seq :]:
         copy.wait_send()
 
 
@@ -541,66 +597,57 @@
         pltpu.VMEM((1, n_mp * LANES), F32),
         pltpu.VMEM((BLOCK, n_mp * LANES), F32),
         pltpu.VMEM((3 * GROUP, n_mp * LANES), BF),
-        pltpu.VMEM((4, LANES, BLOCK), BF),
+        pltpu.VMEM((4, GROUP, BLOCK), BF),
         pltpu.VMEM((1, BLOCK, LANES), F32),
         pltpu.VMEM((8, LANES), F32),
         pltpu.VMEM((n_seq - 1, 8, LANES), F32),
-        pltpu.VMEM((2, width, 2 * LANES), BF),
-        pltpu.VMEM((2, n_dp - 1, chunk, 2 * LANES), BF),
+        pltpu.VMEM((2, n_dp - 1, chunk, BLOCK), BF),
+        pltpu.VMEM((2, n_dp - 1, 2, GROUP, BLOCK), BF),
         pltpu.VMEM((2, n_seq * rows_pad, 2 * LANES), BF),
         pltpu.VMEM((2, n_seq - 1, rows_pad, 2 * LANES), BF),
         pltpu.VMEM((n_mp, BLOCK, LANES), BF),
         pltpu.VMEM((n_mp - 1, BLOCK, LANES), BF),
-        pltpu.VMEM((n_mp, 8, LANES), F32),
-        pltpu.VMEM((n_mp - 1, 8, LANES), F32),
-        pltpu.VMEM((8, LANES), F32),
-        pltpu.VMEM((n_dp - 1, 8, LANES), F32),
-        pltpu.VMEM((8, LANES), F32),
-        pltpu.VMEM((n_seq - 1, 8, LANES), F32),
+        pltpu.VMEM((n_mp, 1, LANES), F32),
+        pltpu.VMEM((n_mp - 1, 1, LANES), F32),
+        pltpu.VMEM((1, LANES), F32),
+        pltpu.VMEM((n_dp - 1, 1, LANES), F32),
         dma((5,)),
     ]
     for shape in (
-        (n_seq // 4, 2, 2, 2), (n_seq // 4, 2, 2, 2), (n_seq - 1,), (2, n_dp - 1), (2, n_seq - 1), (n_mp - 1,),
-        (n_mp - 1,), (n_dp - 1,), (n_seq - 1,),
+        (n_seq // 4, 2, 2, 2), (n_seq // 4, 2, 2, 2), (n_seq - 1,), (2, n_dp - 1), (2, n_dp - 1), (2, n_seq - 1), (n_mp - 1,),
+        (n_mp - 1,), (n_dp - 1,),
     ):
         scratch += [dma(shape), dma(shape)]
-    d_tok, early, late, d_gain = pl.pallas_call(
+    shapes = (
+        jax.ShapeDtypeStruct((GROUP, BLOCK), BF),
+        jax.ShapeDtypeStruct((rows, 3, GROUP), F32),
+        jax.ShapeDtypeStruct((rows, GROUP), F32),
+        jax.ShapeDtypeStruct((1, GROUP), F32),
+    )
+    anywhere = pl.BlockSpec(memory_space=pl.ANY)
+    results = pl.pallas_call(
         functools.partial(layer_kernel, n_seq, n_mp, n_dp),
-        out_shape=(
-            jax.ShapeDtypeStruct((GROUP, BLOCK), BF),
-            jax.ShapeDtypeStruct((rows_pad, 2 * LANES), F32),
-            jax.ShapeDtypeStruct((rows_pad, 2 * LANES), F32),
-            jax.ShapeDtypeStruct((8, LANES), F32),
-        ),
-        in_specs=[pl.BlockSpec(memory_space=pltpu.SMEM)] + [pl.BlockSpec(memory_space=pl.ANY)] * 5,
+        out_shape=shapes,
+        in_specs=[pl.BlockSpec(memory_space=pltpu.SMEM)] + [anywhere] * 5,
         out_specs=(vmem,) * 4,
         scratch_shapes=scratch,
         compiler_params=pltpu.CompilerParams(
             collective_id=0, has_side_effects=True, vmem_limit_bytes=VMEM_BYTES
         ),
     )(counts, tokens[0], grad_out[0], gain, weight, out_weight)
-    tok_turned, d_qkv, out_turned, gain_total = pl.pallas_call(
-        functools.partial(shape_results, rows),
-        out_shape=(
-            jax.ShapeDtypeStruct((GROUP, BLOCK), BF),
-            jax.ShapeDtypeStruct((rows, 3, GROUP), F32),
-            jax.ShapeDtypeStruct((rows, GROUP), F32),
-            jax.ShapeDtypeStruct((GROUP,), F32),
-        ),
+    tok_turned, d_qkv, out_turned, d_gain = pl.pallas_call(
+        hand_on,
+        out_shape=shapes,
         in_specs=[vmem] * 4,
         out_specs=(vmem,) * 4,
         compiler_params=pltpu.CompilerParams(vmem_limit_bytes=VMEM_BYTES),
-    )(d_tok, early, late, d_gain)
-    return (tok_turned.T[None], d_qkv, out_turned.T, gain_total)
-
-
-def shape_results(rows, d_tok, early, late, d_gain, tok_out, qkv_out, out_out, gain_out):
-    tok_out[...] = d_tok[...]
-    qkv_out[:, 0, :] = early[:rows, LANES : LANES + GROUP]
-    qkv_out[:, 1, :] = late[:rows, :GROUP]
-    qkv_out[:, 2, :] = late[:rows, LANES : LANES + GROUP]
-    out_out[...] = early[:rows, :GROUP]
-    gain_out[...] = d_gain[0, :GROUP]
+    )(*results)
+    return (tok_turned.T[None], d_qkv, out_turned.T, d_gain[0])
+
+
+def hand_on(*refs):
+    for at in range(4):
+        refs[4 + at][...] = refs[at][...]
 
 
 def solution(mesh):

time: 71.7 us -> 70.2 us (0.979)
  the two profiles are of different devices: /device:TPU:1 before, /device:TPU:2 now
where the time goes in v3:
time: 70.2 us; the launch traced here: 70 us
  Pallas kernels  68.8 us (98%)
  between operations  1.29 us (2%)
    pallas_call x1, Pallas kernels, per_device(): pl.pallas_call(functools.partial(layer_kernel, n_seq, n_mp, n_dp), out_sh...  67.3 us
    pallas_call x1, Pallas kernels, per_device(): pl.pallas_call(hand_on, out_shape=shapes, in_specs=[vmem] * 4, out_specs=...  1.46 us

profile of v3, /device:TPU:2, one launch (start us, length us, event | category | flops | bytes accessed | tf_op | source)
XLA Modules:
  0.0 70.0 jit_solution(5730576489131667031)
XLA Ops:
  1.3 67.3 %shard_map.93 = (bf16[96,256]{1,0:T(8,128)(2,1)}, f32[12,3,96]{2,1,0:T(4,128)}, f32[12,96]{1,0:T(8,128)}, f32[1,96]{1,0:T(1,128)}) custom-call(s32[1]{0:T(128)S(6)} %copy.10.counts, bf16[256,768]{1,0:T(8,128)(2,1)} %bitcast.11, bf16[256,768]{1,0:T(8,128)(2,1)} %bitcast.12, f32[768]{0:T(1024)} %gain_hbm.1, bf16[288,768]{1,0:T(8,128)(2,1)} %bitcast.10, ...), custom_call_target="tpu_custom_call" | custom-call | tf_op jit(solution)/shard_map/pallas_call | solution.py:628
  68.6 1.5 %shard_map.94 = (bf16[96,256]{1,0:T(8,128)(2,1)}, f32[12,3,96]{2,1,0:T(4,128)}, f32[12,96]{1,0:T(8,128)}, f32[1,96]{1,0:T(1,128)}) custom-call(bf16[96,256]{1,0:T(8,128)(2,1)} %get-tuple-element.12.refs_0_, f32[12,3,96]{2,1,0:T(4,128)} %get-tuple-element.13.refs_1_, f32[12,96]{1,0:T(8,128)} %get-tuple-element.14.refs_2_, f32[1,96]{1,0:T(1,128)} %get-tuple-element.15.refs_3_), custom_call_target="tpu_custom_call" | custom-call | tf_op jit(solution)/shard_map/pallas_call | solution.py:638

commit v4 on v3

--- a/solution.py
+++ b/solution.py
@@ -47,7 +47,8 @@
 def layer_kernel(
     n_seq, n_mp, n_dp,
     counts, tokens_hbm, grad_hbm, gain_hbm, weight_hbm, out_weight_hbm,
-    tok_out, qkv_out, out_out, gain_out,
+    tok_hbm, qkv_hbm, out_hbm, gain_hbm_out,
+    tok_out, qkv_out, out_out, gain_out, out_sem,
     tokens, grad_out, gain, weight, out_weight,
     kv_far, qd_far, scores, probs, scores_t, probs_t, top, kv_here, qd_here, q_rows, da_rows, k_rows, v_rows,
     near_scores, near_probs, normed_s, go_s, normed_p, go_p, gain_pad, form_pad, weight_pad,
@@ -431,21 +432,13 @@
             total = total + z_recv[phase, step - 1].astype(F32)
         return total
 
-    waiting = list(range(stages - 1 - lag, stages))
-    if stages > 1:
-        gather_stage(1, waiting[0])
-    for slot in done:
-        far_terms(slot)
-    if stages > 1:
-        for slot in stage_slots(waiting.pop(0)):
-            turned_scores(slot)
-    for stage in waiting:
+    for stage in range(stages - 1 - lag, stages - 1):
         gather_stage(1, stage)
-    for slot in last:
+    for slot in range(n_seq):
         far_terms(slot)
     near_part()
     y_start(0)
-    for stage in waiting:
+    for stage in range(stages - 1 - lag, stages - 1):
         for slot in stage_slots(stage):
             turned_scores(slot)
 
@@ -461,7 +454,11 @@
 
     key_terms(mid, stat_send[...])
     near_first = far_first[::-1]
-    for step in near_first:
+    for at, step in enumerate(near_first):
+        if at == n_seq - 1 - len(last):
+            gather_stage(1, stages - 1)
+            for slot in last:
+                turned_scores(slot)
         stat_copy(step).wait_recv()
         key_terms((mid - step) % n_seq, stat_recv[step - 1])
     for h in range(2):
@@ -550,6 +547,13 @@
     d_tok = own_parts[0] + (scaled - mean_scaled - form * mean_mixed) * inverse_std
     turned = dot_nt(eye[:LANES, :LANES], d_tok.astype(BF)).astype(BF)
     tok_out[...] = dot_nn(turned, order).astype(BF)[:GROUP, :]
+    stores = [
+        pltpu.make_async_copy(source, target, out_sem.at[at])
+        for at, (source, target) in enumerate((
+            (tok_out, tok_hbm), (qkv_out, qkv_hbm), (out_out, out_hbm), (gain_out, gain_hbm_out),
+        ))
+    ]
+    stores[0].start()
     for copy in started[: 1 - n_seq]:
         copy.wait_send()
     early = z_end(0)
@@ -559,8 +563,12 @@
     qkv_out[:, 1, :] = late[:rows, :GROUP]
     qkv_out[:, 2, :] = late[:rows, LANES : LANES + GROUP]
     gain_out[...] = late[rows : rows + 1, :GROUP] + late[rows : rows + 1, LANES : LANES + GROUP]
+    for store in stores[1:]:
+        store.start()
     for copy in started[1 - n_seq :]:
         copy.wait_send()
+    for store in stores:
+        store.wait()
 
 
 def per_device(n_seq, n_mp, n_dp, tokens, gain, qkv_weight, out_weight, counts, grad_out):
@@ -575,6 +583,11 @@
     far_block = pltpu.VMEM((n_seq, 2 * GROUP, HALF), BF)
     far_square = pltpu.VMEM((2, n_seq, HALF, HALF), F32)
     scratch = [
+        pltpu.VMEM((GROUP, BLOCK), BF),
+        pltpu.VMEM((rows, 3, GROUP), F32),
+        pltpu.VMEM((rows, GROUP), F32),
+        pltpu.VMEM((1, GROUP), F32),
+        dma((4,)),
         pltpu.VMEM((BLOCK, width), BF),
         pltpu.VMEM((BLOCK, width), BF),
         pltpu.VMEM((width,), F32),
@@ -629,7 +642,7 @@
         functools.partial(layer_kernel, n_seq, n_mp, n_dp),
         out_shape=shapes,
         in_specs=[pl.BlockSpec(memory_space=pltpu.SMEM)] + [anywhere] * 5,
-        out_specs=(vmem,) * 4,
+        out_specs=(anywhere,) * 4,
         scratch_shapes=scratch,
         compiler_params=pltpu.CompilerParams(
             collective_id=0, has_side_effects=True, vmem_limit_bytes=VMEM_BYTES

time: 70.2 us -> 68.3 us (0.973)
  the two profiles are of different devices: /device:TPU:2 before, /device:TPU:32 now
where the time goes in v4:
time: 68.3 us; the launch traced here: 68.1 us
  Pallas kernels  66.8 us (98%)
  between operations  1.29 us (2%)
    pallas_call x1, Pallas kernels, per_device(): pl.pallas_call(functools.partial(layer_kernel, n_seq, n_mp, n_dp), out_sh...  65.3 us
    pallas_call x1, Pallas kernels, per_device(): pl.pallas_call(hand_on, out_shape=shapes, in_specs=[vmem] * 4, out_specs=...  1.46 us

profile of v4, /device:TPU:32, one launch (start us, length us, event | category | flops | bytes accessed | tf_op | source)
XLA Modules:
  0.0 68.1 jit_solution(7373711623383651047)
XLA Ops:
  1.3 65.3 %shard_map.93 = (bf16[96,256]{1,0:T(8,128)(2,1)}, f32[12,3,96]{2,1,0:T(4,128)}, f32[12,96]{1,0:T(8,128)}, f32[1,96]{1,0:T(1,128)}) custom-call(s32[1]{0:T(128)S(6)} %copy.10.counts, bf16[256,768]{1,0:T(8,128)(2,1)} %bitcast.11, bf16[256,768]{1,0:T(8,128)(2,1)} %bitcast.12, f32[768]{0:T(1024)} %gain_hbm.1, bf16[288,768]{1,0:T(8,128)(2,1)} %bitcast.10, ...), custom_call_target="tpu_custom_call" | custom-call | tf_op jit(solution)/shard_map/pallas_call | solution.py:641
  66.6 1.5 %shard_map.94 = (bf16[96,256]{1,0:T(8,128)(2,1)}, f32[12,3,96]{2,1,0:T(4,128)}, f32[12,96]{1,0:T(8,128)}, f32[1,96]{1,0:T(1,128)}) custom-call(bf16[96,256]{1,0:T(8,128)(2,1)} %get-tuple-element.12.refs_0_, f32[12,3,96]{2,1,0:T(4,128)} %get-tuple-element.13.refs_1_, f32[12,96]{1,0:T(8,128)} %get-tuple-element.14.refs_2_, f32[1,96]{1,0:T(1,128)} %get-tuple-element.15.refs_3_), custom_call_target="tpu_custom_call" | custom-call | tf_op jit(solution)/shard_map/pallas_call | solution.py:651
